TPU v7x, 256 devices: a whole 4x4x8 slice. The times are simulated.
256 devices in a mesh: sec: 2 (over y_hi), dp: 16 (over x, y_lo, core), tp: 8 (over z).
Axes of the slice: x: 4, y: 4 (y_hi: 2, y_lo: 2; y = y_hi * 2 + y_lo), z: 8, core: 2. Of those that a mesh axis runs over, the one named last changes fastest.
Arguments:
- latents: bfloat16 [256, 64, 1280], P(('dp', 'tp')), may hold values from -6 to 6
- timesteps: int32 [256], P(('dp', 'tp')), may hold values from 0 to 24
- prompt_ids: int32 [256], P(('dp', 'tp')), may hold values from 0 to 63
- prompt_table: bfloat16 [64, 1280], replicated, may hold values from -6 to 6
- gains: float32 [2, 1280], replicated, may hold values from 0.5 to 1.5
- w_in: bfloat16 [2, 1280, 5120], P('sec', None, 'tp'), may hold values from -0.15625 to 0.15625
- w_out: bfloat16 [2, 1280, 5120], P('sec', None, 'tp'), may hold values from -0.078125 to 0.078125
Outputs:
- grad_in: float32 [1280, 5120], P(('sec', 'dp'), 'tp')
- grad_out: float32 [1280, 5120], P(('sec', 'dp'), 'tp')
All inputs are finite; a program needn't handle non-finite values.
Results may differ from a plain program's by a relative error of at most 0.03.
Values may be sent and summed in bfloat16 or wider, within the bound.
A program may use at most 64 MiB of HBM per device.

v0:
```python
import math

import jax
import jax.numpy as jnp
from jax import lax
from jax.sharding import PartitionSpec as P

STEPS = 50


EPS = 1e-06


def shifted(value, axis, steps):
    count = lax.axis_size(axis)
    leading, last = (max(0, -steps), min(count, count - steps))
    return lax.ppermute(value, axis, [(source, source + steps) for source in range(leading, last)])


def gelu_slope(value):
    return 0.5 * (1.0 + lax.erf(value / math.sqrt(2.0))) + value * jnp.exp(
        -0.5 * value * value
    ) / math.sqrt(2.0 * math.pi)


def normed(rows, gain):
    scale = lax.rsqrt(jnp.mean(rows * rows, axis=-1, keepdims=True) + EPS)
    return ((rows * scale * gain).astype(jnp.bfloat16), scale)


def score_of(pooled, text):
    unit_img = pooled * lax.rsqrt(jnp.mean(pooled * pooled, axis=-1, keepdims=True) + EPS)
    unit_txt = text * lax.rsqrt(jnp.mean(text * text, axis=-1, keepdims=True) + EPS)
    return 100.0 * jnp.sum(unit_img * unit_txt, axis=-1) / pooled.shape[-1]


def collect(piece):
    return lax.all_gather(piece, "tp", axis=0, tiled=True)


def reduce_rows(term_fn, local_rows):
    return lax.psum_scatter(
        term_fn(jnp.int32(0), local_rows * lax.axis_size("tp")).astype(jnp.bfloat16),
        "tp",
        scatter_dimension=0,
        tiled=True,
    ).astype(jnp.float32)


def guarded(active, compute, empty):
    return lax.cond(active, compute, empty)


def forward(rows, gain, weight_in, weight_out, active):
    count, tokens, width = rows.shape
    hidden = weight_in.shape[1]
    local_rows = count * tokens
    whole = collect(rows).reshape(-1, width)
    total_rows = whole.shape[0]

    def compute():
        xn, unused = normed(whole.astype(jnp.float32), gain)
        hp = jnp.dot(xn, weight_in, preferred_element_type=jnp.float32)
        return (xn, hp, jax.nn.gelu(hp, approximate=False).astype(jnp.bfloat16))

    def skip():
        return (
            jnp.zeros((total_rows, width), jnp.bfloat16),
            jnp.zeros((total_rows, hidden), jnp.float32),
            jnp.zeros((total_rows, hidden), jnp.bfloat16),
        )

    xn, hp, act = guarded(active, compute, skip)

    def term(start, size):

        def term_product():
            return lax.dot_general(
                act, weight_out, (((1,), (1,)), ((), ())), preferred_element_type=jnp.float32
            )

        return guarded(active, term_product, lambda: jnp.zeros((size, width), jnp.float32))

    mixed = reduce_rows(term, local_rows)
    return (mixed.reshape(count, tokens, width), xn, hp, act)


def reward_back(arrived, mix1, hp1, ids, prompt_table, gain, weight_in, weight_out, active):
    count, tokens, width = arrived.shape
    hidden = weight_in.shape[1]
    local_rows = count * tokens
    seen = arrived.astype(jnp.float32)
    pooled = jnp.mean(seen + mix1, axis=1)
    onehot = (ids[:, None] == jnp.arange(prompt_table.shape[0], dtype=jnp.int32)[None, :]).astype(
        jnp.bfloat16
    )
    text = jnp.dot(onehot, prompt_table, preferred_element_type=jnp.float32)
    g_pooled = jax.grad(lambda p: -jnp.sum(score_of(p, text)))(pooled)
    g_mean = g_pooled / tokens
    all_tok = collect(g_mean.astype(jnp.bfloat16))
    total_rows = hp1.shape[0]

    def grad_hidden():
        g_h = jnp.dot(all_tok, weight_out, preferred_element_type=jnp.float32)
        slope = gelu_slope(hp1).reshape(-1, tokens, hidden)
        return (g_h[:, None, :] * slope).reshape(total_rows, hidden).astype(jnp.bfloat16)

    g_hp1 = guarded(active, grad_hidden, lambda: jnp.zeros((total_rows, hidden), jnp.bfloat16))

    def back_term(start, size):

        def back_product():
            return lax.dot_general(
                g_hp1, weight_in, (((1,), (1,)), ((), ())), preferred_element_type=jnp.float32
            )

        return guarded(active, back_product, lambda: jnp.zeros((size, width), jnp.float32))

    g_xn = reduce_rows(back_term, local_rows)
    flat_seen = seen.reshape(local_rows, width)
    scale1 = lax.rsqrt(jnp.mean(flat_seen * flat_seen, axis=-1, keepdims=True) + EPS)
    weighted = gain * g_xn
    g_norm = scale1 * weighted - flat_seen * scale1**3 * jnp.mean(
        flat_seen * weighted, axis=-1, keepdims=True
    )
    return (g_mean[:, None, :] + g_norm.reshape(count, tokens, width)).astype(jnp.bfloat16)


def weight_terms(g_all, xn0, hp0, act0, weight_out):
    contract_first = (((0,), (0,)), ((), ()))
    grad_w_out = lax.dot_general(g_all, act0, contract_first, preferred_element_type=jnp.float32)
    g_hp0 = (
        jnp.dot(g_all, weight_out, preferred_element_type=jnp.float32) * gelu_slope(hp0)
    ).astype(jnp.bfloat16)
    grad_w_in = lax.dot_general(xn0, g_hp0, contract_first, preferred_element_type=jnp.float32)
    return (grad_w_in, grad_w_out)


def on_device(latents, timesteps, prompt_ids, prompt_table, gains, w_in, w_out):
    count, tokens, width = latents.shape
    hidden = w_in.shape[2]
    segment = lax.axis_index("sec")
    diffusing = segment == 0
    scoring = segment == 1
    weight_in = w_in[0]
    weight_out = w_out[0]
    theta = math.pi / 2.0 * (timesteps.astype(jnp.float32) + 1.0) / (STEPS + 1.0)
    alpha = jnp.cos(theta)[:, None, None]
    sigma = jnp.sin(theta)[:, None, None]
    eps_mix, xn0, hp0, act0 = forward(latents, gains[0], weight_in, weight_out, diffusing)
    base = latents.astype(jnp.float32)
    images = ((base - sigma * (base + eps_mix)) / alpha).astype(jnp.bfloat16)
    arrived = shifted(images, "sec", 1)
    mix1, xn1, hp1, act1 = forward(arrived, gains[1], weight_in, weight_out, scoring)
    g_images = reward_back(
        arrived, mix1, hp1, prompt_ids, prompt_table, gains[1], weight_in, weight_out, scoring
    )
    returned = shifted(g_images, "sec", -1)
    g_eps = (-(sigma / alpha) * returned.astype(jnp.float32)).astype(jnp.bfloat16)
    g_all = collect(g_eps).reshape(-1, width)

    def no_terms():
        return (jnp.zeros((width, hidden), jnp.float32), jnp.zeros((width, hidden), jnp.float32))

    grad_w_in, grad_w_out = lax.cond(
        diffusing, lambda: weight_terms(g_all, xn0, hp0, act0, weight_out), no_terms
    )
    grad_in, grad_out = (
        lax.psum_scatter(
            grad_w_in.astype(jnp.bfloat16), ("sec", "dp"), scatter_dimension=0, tiled=True
        ).astype(jnp.float32),
        lax.psum_scatter(
            grad_w_out.astype(jnp.bfloat16), ("sec", "dp"), scatter_dimension=0, tiled=True
        ).astype(jnp.float32),
    )
    return (grad_in, grad_out)


def solution(mesh):
    in_specs = (
        P(("dp", "tp"), None, None),
        P(("dp", "tp")),
        P(("dp", "tp")),
        P(),
        P(),
        P("sec", None, "tp"),
        P("sec", None, "tp"),
    )
    out_specs = (P(("sec", "dp"), "tp"), P(("sec", "dp"), "tp"))
    return jax.shard_map(
        on_device, mesh=mesh, in_specs=in_specs, out_specs=out_specs, check_vma=False
    )
```

profile of v0, /device:TPU:32, one launch (start us, length us, event | category | flops | bytes accessed | tf_op | source)
XLA Modules:
  0.0 666.1 jit_solution(10509796451165419809)
XLA Ops:
  8.0 46.6 %all-gather.5.cloned.1.call-done = bf16[16,64,1280]{2,1,0:T(8,128)(2,1)} async-done(((bf16[2,64,1280]{2,1,0:T(8,128)(2,1)}), bf16[16,64,1280]{2,1,0:T(8,128)(2,1)}) %all-gather.5.cloned.1.call-update) | async-done | bytes 2621456 | tf_op jit(solution)/shard_map/all_gather | solution.py:38
  54.6 14.8 %conditional.7 = (bf16[1024,1280]{1,0:T(8,128)(2,1)}, f32[1024,640]{1,0:T(8,128)}, bf16[1024,640]{1,0:T(8,128)(2,1)}) conditional(s32[]{:T(128)} %convert_element_type.98, () %tuple.58, (bf16[16,64,1280]{2,1,0:T(8,128)(2,1)}, f32[2,1280]{1,0:T(2,128)}, bf16[1280,640]{1,0:T(8,128)(2,1)}) %tuple.117), branch_computations={%region_1.2_spmd, %region_2.4_spmd} | conditional | flops 1729496064 | bytes 33176684 | solution.py:51
  54.6 2.5 multiply_reduce_fusion
  57.2 2.2 fusion.18
  59.4 10.0 %fusion.21 = (bf16[1024,640]{1,0:T(8,128)(2,1)}, f32[1024,640]{1,0:T(8,128)}) fusion(bf16[1024,1280]{1,0:T(8,128)(2,1)} %fusion.18, bf16[1280,640]{1,0:T(8,128)(2,1)S(1)} %copy-done.14), kind=kOutput, calls=%fused_computation.27 | convolution fusion | flops 1720320000 | bytes 8192000 | tf_op jit(solution)/shard_map/cond/branch_1_fun/dot_general | solution.py:63
  69.4 4.1 conditional.8
  69.4 4.1 fusion.60
  73.5 1.5 copy-done.3
  75.1 40.7 %reduce-scatter.12.cloned.1.call-done = bf16[128,1280]{1,0:T(8,128)(2,1)} async-done(((bf16[1024,1280]{1,0:T(8,128)(2,1)}), bf16[128,1280]{1,0:T(8,128)(2,1)}) %reduce-scatter.12.cloned.1.call-update) | async-done | bytes 327696 | tf_op jit(solution)/shard_map/reduce_scatter | solution.py:42
  117.0 4.4 collective-permute-start
  121.4 4.6 collective-permute-done
  126.8 43.6 %all-gather.7.cloned.1.call-done = bf16[16,64,1280]{2,1,0:T(8,128)(2,1)} async-done(((bf16[2,64,1280]{2,1,0:T(8,128)(2,1)}), bf16[16,64,1280]{2,1,0:T(8,128)(2,1)}) %all-gather.7.cloned.1.call-update) | async-done | bytes 2621456 | tf_op jit(solution)/shard_map/all_gather | solution.py:38
  170.4 3.0 conditional.9
  170.4 1.8 broadcast.329
  172.2 1.2 broadcast.330
  173.8 1.5 copy-done.4
  175.7 54.7 %reduce-scatter.14.cloned.1.call-done = bf16[128,1280]{1,0:T(8,128)(2,1)} async-done(((bf16[1024,1280]{1,0:T(8,128)(2,1)}), bf16[128,1280]{1,0:T(8,128)(2,1)}) %reduce-scatter.14.cloned.1.call-update) | async-done | bytes 327696 | tf_op jit(solution)/shard_map/reduce_scatter | solution.py:42
  231.9 24.6 %all-gather = bf16[8,2,1280]{2,1,0:T(2,128)(2,1)S(1)} all-gather(bf16[1,2,1280]{2,1,0:T(2,128)(2,1)S(1)} %get-tuple-element.101), channel_id=1, replica_groups=mesh['sec'=2,'dp'=16,'tp'=8] {'tp'}, dimensions={0}, use_global_device_ids=true | all-gather | bytes 46080 | tf_op jit(solution)/shard_map/all_gather | solution.py:38
  256.8 1.5 copy-done.5
  258.5 52.8 %reduce-scatter.16.cloned.1.call-done = bf16[128,1280]{1,0:T(8,128)(2,1)} async-done(((bf16[1024,1280]{1,0:T(8,128)(2,1)}), bf16[128,1280]{1,0:T(8,128)(2,1)}) %reduce-scatter.16.cloned.1.call-update) | async-done | bytes 327696 | tf_op jit(solution)/shard_map/reduce_scatter | solution.py:42
  312.5 1.2 fusion.46
  313.8 1.3 collective-permute-start.1
  315.1 9.2 %collective-permute-done.1 = bf16[2,64,1280]{2,1,0:T(8,128)(2,1)S(1)} collective-permute-done((bf16[2,64,1280]{2,1,0:T(8,128)(2,1)S(1)}, bf16[2,64,1280]{2,1,0:T(8,128)(2,1)S(1)}, u32[]{:S(2)}, u32[]{:S(2)}) %collective-permute-start.1) | collective-permute-done | bytes 327712 | tf_op jit(solution)/shard_map/ppermute | solution.py:17
  325.2 41.0 %all-gather.9.cloned.1.call-done = bf16[16,64,1280]{2,1,0:T(8,128)(2,1)} async-done(((bf16[2,64,1280]{2,1,0:T(8,128)(2,1)}), bf16[16,64,1280]{2,1,0:T(8,128)(2,1)}) %all-gather.9.cloned.1.call-update) | async-done | bytes 2621456 | tf_op jit(solution)/shard_map/all_gather | solution.py:38
  366.2 15.2 %conditional.13 = (bf16[1280,640]{0,1:T(8,128)(2,1)S(1)}, bf16[1280,640]{1,0:T(8,128)(2,1)S(1)}) conditional(s32[]{:T(128)} %convert_element_type.98, () %tuple.56, (bf16[16,64,1280]{2,1,0:T(8,128)(2,1)}, bf16[1280,640]{1,0:T(8,128)(2,1)}, f32[1024,640]{1,0:T(8,128)}, bf16[1024,1280]{1,0:T(8,128)(2,1)}, bf16[1024,640]{1,0:T(8,128)(2,1)}) %tuple.116), branch_computations={%region_23.0_spmd, %region_24.0_spmd} | conditional | flops 5039718400 | bytes 16711696 | solution.py:165
  366.2 10.9 %convolution_bitcast_fusion = bf16[1280,640]{0,1:T(8,128)(2,1)S(1)} fusion(bf16[1024,1280]{1,0:T(8,128)(2,1)} %get-tuple-element.74, f32[1024,640]{1,0:T(8,128)} %get-tuple-element.73, bf16[1024,1280]{1,0:T(8,128)(2,1)} %bitcast.61, bf16[1280,640]{1,0:T(8,128)(2,1)} %get-tuple-element.72), kind=kOutput, calls=%fused_computation.8 | convolution fusion | flops 3361996800 | bytes 11141120 | tf_op jit(solution)/shard_map/cond/branch_1_fun/dot_general | solution.py:135
  377.1 4.4 fusion.64
  381.4 2.4 copy.12
  384.6 135.3 %reduce-scatter.18.cloned.1.call-done = bf16[40,640]{1,0:T(8,128)(2,1)} async-done(((bf16[1280,640]{1,0:T(8,128)(2,1)}), bf16[40,640]{1,0:T(8,128)(2,1)}) %reduce-scatter.18.cloned.1.call-update) | async-done | bytes 51216
  519.9 1.5 convert_element_type.113
  521.3 136.4 %reduce-scatter.20.cloned.1.call-done = bf16[40,640]{1,0:T(8,128)(2,1)} async-done(((bf16[1280,640]{1,0:T(8,128)(2,1)}), bf16[40,640]{1,0:T(8,128)(2,1)}) %reduce-scatter.20.cloned.1.call-update) | async-done | bytes 51216
  657.8 1.5 convert_element_type.115
  (66 shorter events, 9.1 us)
Async XLA Ops:
  7.2 168.2 %copy-start = (bf16[64,1280]{1,0:T(8,128)(2,1)S(1)}, bf16[64,1280]{1,0:T(8,128)(2,1)}, u32[]{:S(2)}) copy-start(bf16[64,1280]{1,0:T(8,128)(2,1)} %param.24) | copy-start | bytes 491524
  7.2 47.4 %all-gather.5.cloned.1.call-start = ((), (), s32[]{:S(2)}) async-start(), calls=%async_computation.5 | async-start | bytes 2949120 | tf_op jit(solution)/shard_map/all_gather | solution.py:38
  7.9 107.9 %reduce-scatter.12.cloned.1.call-start = ((), (), s32[]{:S(2)}) async-start(), calls=%async_computation.6 | async-start | bytes 2949120 | tf_op jit(solution)/shard_map/reduce_scatter | solution.py:42
  54.6 2.6 copy-start.12
  54.6 2.6 copy-start.1
  57.2 2.2 copy-start.14
  73.4 1.5 copy-start.3
  73.4 1.6 copy-start.13
  73.4 42.3 %copy-start.10 = (bf16[2,64,1280]{2,1,0:T(8,128)(2,1)S(1)}, bf16[2,64,1280]{2,1,0:T(8,128)(2,1)}, u32[]{:S(2)}) copy-start(bf16[2,64,1280]{2,1,0:T(8,128)(2,1)} %param.21) | copy-start | bytes 983044
  73.5 53.3 %copy-start.11 = (f32[2,1280]{1,0:T(2,128)S(1)}, f32[2,1280]{1,0:T(2,128)}, u32[]{:S(2)}) copy-start(f32[2,1280]{1,0:T(2,128)} %param.25) | copy-start | bytes 30724
  75.0 95.5 %all-gather.7.cloned.1.call-start = ((), (), s32[]{:S(2)}) async-start(), calls=%async_computation.7 | async-start | bytes 2949120 | tf_op jit(solution)/shard_map/all_gather | solution.py:38
  117.0 9.0 %collective-permute-start = (bf16[2,64,1280]{2,1,0:T(8,128)(2,1)S(1)}, bf16[2,64,1280]{2,1,0:T(8,128)(2,1)S(1)}, u32[]{:S(2)}, u32[]{:S(2)}) collective-permute-start(bf16[2,64,1280]{2,1,0:T(8,128)(2,1)S(1)} %fusion.48), channel_id=1, source_target_pairs={{0,128},{1,129},{2,130},{3,131},{4,132},{5,133},{6,134},{7,135},{8... | collective-permute-start | bytes 983048 | tf_op jit(solution)/shard_map/ppermute | solution.py:17
  126.0 0.7 copy-start.7
  126.7 103.7 %reduce-scatter.14.cloned.1.call-start = ((), (), s32[]{:S(2)}) async-start(), calls=%async_computation.8 | async-start | bytes 2949120 | tf_op jit(solution)/shard_map/reduce_scatter | solution.py:42
  173.8 1.5 copy-start.4
  173.8 1.6 copy-start.16
  173.8 56.6 %copy-start.8 = (bf16[2,64,1280]{2,1,0:T(8,128)(2,1)S(1)}, bf16[2,64,1280]{2,1,0:T(8,128)(2,1)}, u32[]{:S(2)}) copy-start(bf16[2,64,1280]{2,1,0:T(8,128)(2,1)} %copy-done.7) | copy-start | bytes 983044
  175.3 136.0 %reduce-scatter.16.cloned.1.call-start = ((), (), s32[]{:S(2)}) async-start(), calls=%async_computation.9 | async-start | bytes 2949120 | tf_op jit(solution)/shard_map/reduce_scatter | solution.py:42
  256.8 1.5 copy-start.5
  258.4 107.8 %all-gather.9.cloned.1.call-start = ((), (), s32[]{:S(2)}) async-start(), calls=%async_computation.10 | async-start | bytes 2949120 | tf_op jit(solution)/shard_map/all_gather | solution.py:38
  313.8 10.5 %collective-permute-start.1 = (bf16[2,64,1280]{2,1,0:T(8,128)(2,1)S(1)}, bf16[2,64,1280]{2,1,0:T(8,128)(2,1)S(1)}, u32[]{:S(2)}, u32[]{:S(2)}) collective-permute-start(bf16[2,64,1280]{2,1,0:T(8,128)(2,1)S(1)} %add_convert_fusion), channel_id=1, source_target_pairs={{128,0},{129,1},{130,2},{131,3},{132,4},{133,5},{134,6},{135,7},{1... | collective-permute-start | bytes 983048 | tf_op jit(solution)/shard_map/ppermute | solution.py:17
  325.2 194.7 %reduce-scatter.18.cloned.1.call-start = ((), (), s32[]{:S(2)}) async-start(), calls=%async_computation.11 | async-start | bytes 1689600
  381.4 2.4 copy-start.6
  383.8 274.0 %reduce-scatter.20.cloned.1.call-start = ((), (), s32[]{:S(2)}) async-start(), calls=%async_computation.12 | async-start | bytes 1689600
Sparse Core Ops, SparseCore 0:
  9.8 44.7 all-gather.4
  75.1 40.6 reduce-scatter.11
  126.9 43.5 all-gather.6
  175.5 54.9 reduce-scatter.13
  258.5 52.8 reduce-scatter.15
  325.3 40.8 all-gather.8
  383.9 135.9 reduce-scatter.17
  522.6 135.1 reduce-scatter.19
where the time goes:
time: 667 us; the launch traced here: 666 us
  waiting for transfers between devices  566 us (85%)
  matrix products  29.6 us (4%)
  blocking collectives  24.6 us (4%)
  between operations  14.4 us (2%)
  other arithmetic  13.6 us (2%)
  local copies, waits for them, and re-layouts  11.2 us (2%)
    unnamed x10, waiting for transfers between devices  273 us
    reduce_scatter x3, waiting for transfers between devices, reduce_rows(): lax.psum_scatter(term_fn(jnp.int32(0), local_rows * lax.axis_size('tp'))....  148 us
    all_gather x3, waiting for transfers between devices, collect(): return lax.all_gather(piece, 'tp', axis=0, tiled=True)  131 us
    all_gather x1, blocking collectives, collect(): return lax.all_gather(piece, 'tp', axis=0, tiled=True)  24.6 us
    ppermute x2, waiting for transfers between devices, shifted(): lax.ppermute(value, axis, [(source, source + steps) for source in range(l...  13.7 us
  transfers between devices with their start and end apart: 10, of which 10 were waited for; matrix products, arithmetic and copies ran while one was open for 0% of the time, Pallas kernels for 0%

commit v1 on v0

v1 whole, which is shorter than its diff:
```python
import math

import jax
import jax.numpy as jnp
from jax import lax
from jax.sharding import PartitionSpec as P

STEPS = 50
EPS = 1e-06


def gelu_slope(value):
    return 0.5 * (1.0 + lax.erf(value / math.sqrt(2.0))) + value * jnp.exp(
        -0.5 * value * value
    ) / math.sqrt(2.0 * math.pi)


def normed(rows, gain):
    scale = lax.rsqrt(jnp.mean(rows * rows, axis=-1, keepdims=True) + EPS)
    return ((rows * scale * gain).astype(jnp.bfloat16), scale)


def score_of(pooled, text):
    unit_img = pooled * lax.rsqrt(jnp.mean(pooled * pooled, axis=-1, keepdims=True) + EPS)
    unit_txt = text * lax.rsqrt(jnp.mean(text * text, axis=-1, keepdims=True) + EPS)
    return 100.0 * jnp.sum(unit_img * unit_txt, axis=-1) / pooled.shape[-1]


def collect(piece):
    return lax.all_gather(piece, "tp", axis=0, tiled=True)


def reduce_rows(value):
    return lax.psum_scatter(value, "tp", scatter_dimension=0, tiled=True).astype(jnp.float32)


def contract_last(left, right):
    return lax.dot_general(left, right, (((1,), (1,)), ((), ())), preferred_element_type=jnp.float32)


def contract_first(left, right):
    return lax.dot_general(left, right, (((0,), (0,)), ((), ())), preferred_element_type=jnp.float32)


def on_device(latents, timesteps, prompt_ids, prompt_table, gains, w_in, w_out):
    count, tokens, width = latents.shape
    segment = lax.axis_index("sec")
    swap = [(0, 1), (1, 0)]
    other_in = lax.ppermute(w_in[0], "sec", swap)
    other_out = lax.ppermute(w_out[0], "sec", swap)
    first = segment == 0
    win0 = jnp.where(first, w_in[0], other_in)
    wout0 = jnp.where(first, w_out[0], other_out)
    win1 = jnp.where(first, other_in, w_in[0])
    wout1 = jnp.where(first, other_out, w_out[0])
    own = lax.dynamic_index_in_dim(latents, segment, 0, keepdims=False)
    step = lax.dynamic_index_in_dim(timesteps, segment, 0, keepdims=False)
    prompt = lax.dynamic_index_in_dim(prompt_ids, segment, 0, keepdims=True)
    theta = math.pi / 2.0 * (step.astype(jnp.float32) + 1.0) / (STEPS + 1.0)
    alpha, sigma = jnp.cos(theta), jnp.sin(theta)

    xn0, _ = normed(collect(own).astype(jnp.float32), gains[0])
    hp0 = jnp.dot(xn0, win0, preferred_element_type=jnp.float32)
    act0 = jax.nn.gelu(hp0, approximate=False).astype(jnp.bfloat16)
    mix0 = reduce_rows(contract_last(act0, wout0).astype(jnp.bfloat16))
    base = own.astype(jnp.float32)
    images = ((base - sigma * (base + mix0)) / alpha).astype(jnp.bfloat16)

    seen = images.astype(jnp.float32)
    xn1, _ = normed(collect(images).astype(jnp.float32), gains[1])
    hp1 = jnp.dot(xn1, win1, preferred_element_type=jnp.float32)
    act1 = jax.nn.gelu(hp1, approximate=False).astype(jnp.bfloat16).astype(jnp.float32)
    mean1 = jnp.mean(act1.reshape(-1, tokens, act1.shape[-1]), axis=1)
    high = mean1.astype(jnp.bfloat16)
    low = (mean1 - high.astype(jnp.float32)).astype(jnp.bfloat16)
    mix1 = reduce_rows(contract_last(high, wout1) + contract_last(low, wout1))
    pooled = jnp.mean(seen, axis=0, keepdims=True) + mix1
    onehot = (prompt[:, None] == jnp.arange(prompt_table.shape[0], dtype=jnp.int32)[None, :]).astype(
        jnp.bfloat16
    )
    text = jnp.dot(onehot, prompt_table, preferred_element_type=jnp.float32)
    g_mean = jax.grad(lambda p: -jnp.sum(score_of(p, text)))(pooled) / tokens
    all_tok = collect(g_mean.astype(jnp.bfloat16))
    g_h1 = jnp.dot(all_tok, wout1, preferred_element_type=jnp.float32)
    slope1 = gelu_slope(hp1).reshape(-1, tokens, hp1.shape[-1])
    g_hp1 = (g_h1[:, None, :] * slope1).reshape(hp1.shape).astype(jnp.bfloat16)
    g_xn = reduce_rows(contract_last(g_hp1, win1).astype(jnp.bfloat16))
    scale1 = lax.rsqrt(jnp.mean(seen * seen, axis=-1, keepdims=True) + EPS)
    weighted = gains[1] * g_xn
    g_norm = scale1 * weighted - seen * scale1**3 * jnp.mean(seen * weighted, axis=-1, keepdims=True)
    g_images = (g_mean + g_norm).astype(jnp.bfloat16)
    g_eps = (-(sigma / alpha) * g_images.astype(jnp.float32)).astype(jnp.bfloat16)

    g_all = collect(g_eps)
    grad_w_out = contract_first(g_all, act0)
    g_hp0 = (jnp.dot(g_all, wout0, preferred_element_type=jnp.float32) * gelu_slope(hp0)).astype(
        jnp.bfloat16
    )
    grad_w_in = contract_first(xn0, g_hp0)
    return tuple(
        lax.psum_scatter(
            value.astype(jnp.bfloat16), ("sec", "dp"), scatter_dimension=0, tiled=True
        ).astype(jnp.float32)
        for value in (grad_w_in, grad_w_out)
    )


def solution(mesh):
    in_specs = (
        P(("dp", "tp"), None, None),
        P(("dp", "tp")),
        P(("dp", "tp")),
        P(),
        P(),
        P("sec", None, "tp"),
        P("sec", None, "tp"),
    )
    out_specs = (P(("sec", "dp"), "tp"), P(("sec", "dp"), "tp"))
    return jax.shard_map(
        on_device, mesh=mesh, in_specs=in_specs, out_specs=out_specs, check_vma=False
    )
```

time: 667 us -> 606 us (0.909)
  waiting for transfers between devices: 566 us -> 478 us
  blocking collectives: 24.6 us -> 51.8 us
    reduce_scatter x3 -> x2, waiting for transfers between devices: 148 us -> 78.5 us  [reduce_rows(): lax.psum_scatter(value, 'tp', scatter_dimension=0, tiled=True)]
    unnamed x0 -> x1, blocking collectives: none -> 27.2 us
    all_gather x3, waiting for transfers between devices: 131 us -> 109 us  [collect(): return lax.all_gather(piece, 'tp', axis=0, tiled=True)]
    ppermute x2, waiting for transfers between devices: 13.7 us -> 22.8 us  [the longest x1 22.8 us: on_device(): other_out = lax.ppermute(w_out[0], 'sec', swap)]
    unnamed x10 -> x9, waiting for transfers between devices: 273 us -> 267 us
    dot_general x5 -> x10, matrix products: 29.6 us -> 31 us  [the longest x2 9.55 us: contract_first(): lax.dot_general(left, right, (((0,), (0,)), ((), ())), preferred_element_...]
  transfers between devices with their start and end apart: 10 -> 9, of which waited for: 10 -> 8; matrix products, arithmetic and copies ran while one was open for 0% -> 3% of each run, Pallas kernels for 0% -> 0%
where the time goes in v1:
time: 606 us; the launch traced here: 605 us
  waiting for transfers between devices  478 us (79%)
  blocking collectives  51.8 us (9%)
  matrix products  31 us (5%)
  between operations  17.3 us (3%)
  other arithmetic  15 us (2%)
  local copies, waits for them, and re-layouts  8.34 us (1%)
    unnamed x9, waiting for transfers between devices  267 us
    all_gather x3, waiting for transfers between devices, collect(): return lax.all_gather(piece, 'tp', axis=0, tiled=True)  109 us
    reduce_scatter x2, waiting for transfers between devices, reduce_rows(): lax.psum_scatter(value, 'tp', scatter_dimension=0, tiled=True)  78.5 us
    unnamed x1, blocking collectives  27.2 us
    all_gather x1, blocking collectives, collect(): return lax.all_gather(piece, 'tp', axis=0, tiled=True)  24.6 us
    ppermute x1, waiting for transfers between devices, on_device(): other_out = lax.ppermute(w_out[0], 'sec', swap)  22.8 us
  transfers between devices with their start and end apart: 9, of which 8 were waited for; matrix products, arithmetic and copies ran while one was open for 3% of the time, Pallas kernels for 0%

profile of v1, /device:TPU:32, one launch (start us, length us, event | category | flops | bytes accessed | tf_op | source)
XLA Modules:
  0.0 605.3 jit_solution(8391144982255607296)
XLA Ops:
  7.2 1.6 constant_dynamic-slice_fusion
  8.9 3.3 collective-permute-start
  12.5 0.8 slice_reduce_fusion
  13.4 37.8 %all-gather.10.cloned.1.call-done = bf16[1,512,1280]{2,1,0:T(8,128)(2,1)} async-done(((bf16[1,64,1280]{2,1,0:T(8,128)(2,1)}), bf16[1,512,1280]{2,1,0:T(8,128)(2,1)}) %all-gather.10.cloned.1.call-update) | async-done | bytes 1310736 | tf_op jit(solution)/shard_map/all_gather | solution.py:30
  51.2 1.7 fusion.3
  53.0 1.2 copy-done.14
  54.1 6.4 %fusion.12 = (bf16[512,640]{1,0:T(8,128)(2,1)S(1)}, f32[512,640]{1,0:T(8,128)}) fusion(bf16[1280,640]{1,0:T(8,128)(2,1)} %copy-done.14, pred[]{:T(512)S(6)} %eq.19, bf16[1,1280,640]{2,1,0:T(8,128)(2,1)} %param.12, bf16[1,512,1280]{2,1,0:T(8,128)(2,1)S(1)} %copy-done.5, f32[1280]{0:T(1024)S(1)} %get-tuple-element.5, f32[512]{0:T(512)S(1)} %add_rsqrt_fusion.1), kind=kOutput, calls=%fused_computation.29 | convolution fusion | flops 863600640 | bytes 6560769 | tf_op jit(solution)/shard_map/dot_general | solution.py:63
  60.5 22.8 %collective-permute-done.1 = bf16[1280,640]{1,0:T(8,128)(2,1)S(1)} collective-permute-done((bf16[1280,640]{1,0:T(8,128)(2,1)}, bf16[1280,640]{1,0:T(8,128)(2,1)S(1)}, u32[]{:S(2)}, u32[]{:S(2)}) %collective-permute-start.1) | collective-permute-done | bytes 1638432 | tf_op jit(solution)/shard_map/ppermute | solution.py:50
  83.4 2.3 convolution_convert_fusion.3
  87.8 39.4 %reduce-scatter.11.cloned.1.call-done = bf16[64,1280]{1,0:T(8,128)(2,1)} async-done(((bf16[512,1280]{1,0:T(8,128)(2,1)}), bf16[64,1280]{1,0:T(8,128)(2,1)}) %reduce-scatter.11.cloned.1.call-update) | async-done | bytes 163856 | tf_op jit(solution)/shard_map/reduce_scatter | solution.py:34
  127.2 1.7 convert_reduce_fusion.1
  129.6 0.8 convolution_reduce_fusion
  132.3 1.6 broadcast_select_fusion
  133.9 33.1 %all-gather.6.cloned.1.call-done = bf16[512,1280]{1,0:T(8,128)(2,1)} async-done(((bf16[64,1280]{1,0:T(8,128)(2,1)}), bf16[512,1280]{1,0:T(8,128)(2,1)}) %all-gather.6.cloned.1.call-update) | async-done | bytes 1310736 | tf_op jit(solution)/shard_map/all_gather | solution.py:30
  167.1 1.7 fusion
  168.8 6.8 %convert_reduce_fusion = (f32[8,640]{1,0:T(8,128)S(1)}, f32[512,640]{1,0:T(8,128)}) fusion(bf16[1280,640]{1,0:T(8,128)(2,1)} %copy-done.14, pred[]{:T(512)S(6)} %eq.19, bf16[1,1280,640]{2,1,0:T(8,128)(2,1)} %param.12, bf16[512,1280]{1,0:T(8,128)(2,1)S(1)} %copy-done.6, f32[1280]{0:T(1024)S(1)} %get-tuple-element.4, f32[512]{0:T(512)S(1)} %add_rsqrt_fusion), kind=kOutput, calls=%fused_computation.44 | convolution fusion | flops 864250880 | bytes 5925889 | tf_op jit(solution)/shard_map/dot_general | solution.py:71
  176.7 27.2 %all-reduce = f32[8,1280]{1,0:T(8,128)S(1)} all-reduce(f32[8,1280]{1,0:T(8,128)S(1)} %convolution_add_fusion), channel_id=4, replica_groups=mesh['sec'=2,'dp'=16,'tp'=8] {'tp'}, use_global_device_ids=true, to_apply=%region_6.7.clone | all-reduce | flops 10240 | bytes 81920
  203.9 1.3 multiply_reduce_fusion.1
  206.8 24.6 %all-gather.1 = bf16[8,1,1280]{2,1,0:T(2,128)(2,1)S(1)} all-gather(bf16[1,1,1280]{2,1,0:T(2,128)(2,1)S(1)} %bitcast.73), channel_id=1, replica_groups=mesh['sec'=2,'dp'=16,'tp'=8] {'tp'}, dimensions={0}, use_global_device_ids=true | all-gather | bytes 23040 | tf_op jit(solution)/shard_map/all_gather | solution.py:30
  232.3 0.9 copy-done.13
  233.2 3.7 convolution_convert_fusion.2
  237.0 39.1 %reduce-scatter.13.cloned.1.call-done = bf16[64,1280]{1,0:T(8,128)(2,1)} async-done(((bf16[512,1280]{1,0:T(8,128)(2,1)}), bf16[64,1280]{1,0:T(8,128)(2,1)}) %reduce-scatter.13.cloned.1.call-update) | async-done | bytes 163856 | tf_op jit(solution)/shard_map/reduce_scatter | solution.py:34
  276.1 1.1 fusion.53
  277.2 1.7 multiply_convert_fusion
  279.0 38.2 %all-gather.8.cloned.1.call-done = bf16[512,1280]{1,0:T(8,128)(2,1)} async-done(((bf16[64,1280]{1,0:T(8,128)(2,1)}), bf16[512,1280]{1,0:T(8,128)(2,1)}) %all-gather.8.cloned.1.call-update) | async-done | bytes 1310736 | tf_op jit(solution)/shard_map/all_gather | solution.py:30
  317.3 3.7 convolution_convert_fusion
  321.1 1.3 copy-done.4
  322.4 5.8 convolution_convert_fusion.1
  328.3 130.7 %reduce-scatter.17.cloned.1.call-done = bf16[40,640]{1,0:T(8,128)(2,1)} async-done(((bf16[1280,640]{1,0:T(8,128)(2,1)}), bf16[40,640]{1,0:T(8,128)(2,1)}) %reduce-scatter.17.cloned.1.call-update) | async-done | bytes 51216
  459.0 1.5 convert_element_type.110
  460.4 136.6 %reduce-scatter.15.cloned.1.call-done = bf16[40,640]{1,0:T(8,128)(2,1)} async-done(((bf16[1280,640]{1,0:T(8,128)(2,1)}), bf16[40,640]{1,0:T(8,128)(2,1)}) %reduce-scatter.15.cloned.1.call-update) | async-done | bytes 51216
  597.0 1.5 convert_element_type.108
  (68 shorter events, 5.9 us)
Async XLA Ops:
  7.2 122.4 %copy-start = (bf16[64,1280]{1,0:T(8,128)(2,1)S(1)}, bf16[64,1280]{1,0:T(8,128)(2,1)}, u32[]{:S(2)}) copy-start(bf16[64,1280]{1,0:T(8,128)(2,1)} %param.10) | copy-start | bytes 491524
  7.2 44.0 %all-gather.10.cloned.1.call-start = ((), (), s32[]{:S(2)}) async-start(), calls=%async_computation.8 | async-start | bytes 1474560 | tf_op jit(solution)/shard_map/all_gather | solution.py:30
  8.9 118.3 %reduce-scatter.11.cloned.1.call-start = ((), (), s32[]{:S(2)}) async-start(), calls=%async_computation.4 | async-start | bytes 1474560 | tf_op jit(solution)/shard_map/reduce_scatter | solution.py:34
  8.9 44.0 %collective-permute-start = (bf16[1280,640]{1,0:T(8,128)(2,1)}, bf16[1280,640]{1,0:T(8,128)(2,1)S(1)}, u32[]{:S(2)}, u32[]{:S(2)}) collective-permute-start(bf16[1280,640]{1,0:T(8,128)(2,1)} %bitcast.74), channel_id=1, source_target_pairs={{0,128},{128,0},{1,129},{129,1},{2,130},{130,2},{3,131},{131,3},{4... | collective-permute-start | bytes 4915208 | tf_op jit(solution)/shard_map/ppermute | solution.py:49
  12.2 71.2 %collective-permute-start.1 = (bf16[1280,640]{1,0:T(8,128)(2,1)}, bf16[1280,640]{1,0:T(8,128)(2,1)S(1)}, u32[]{:S(2)}, u32[]{:S(2)}) collective-permute-start(bf16[1280,640]{1,0:T(8,128)(2,1)} %bitcast.72), channel_id=1, source_target_pairs={{0,128},{128,0},{1,129},{129,1},{2,130},{130,2},{3,131},{131,3},{4... | collective-permute-start | bytes 4915208 | tf_op jit(solution)/shard_map/ppermute | solution.py:50
  13.3 47.2 %copy-start.9 = (f32[1280]{0:T(1024)}, f32[1280]{0:T(1024)S(1)}, u32[]{:S(2)}) copy-start(f32[1280]{0:T(1024)S(1)} %get-tuple-element.5) | copy-start | bytes 15364
  51.2 3.0 copy-start.5
  52.9 7.6 %copy-start.11 = (f32[512]{0:T(512)}, f32[512]{0:T(512)S(1)}, u32[]{:S(2)}) copy-start(f32[512]{0:T(512)S(1)} %add_rsqrt_fusion.1) | copy-start | bytes 6148
  52.9 1.2 copy-start.14
  54.1 29.2 %copy-start.2 = (bf16[1,1280,640]{2,1,0:T(8,128)(2,1)S(1)}, bf16[1,1280,640]{2,1,0:T(8,128)(2,1)}, u32[]{:S(2)}) copy-start(bf16[1,1280,640]{2,1,0:T(8,128)(2,1)} %param.13) | copy-start | bytes 4915204
  60.5 22.8 %copy-start.18 = (bf16[512,640]{1,0:T(8,128)(2,1)}, bf16[512,640]{1,0:T(8,128)(2,1)S(1)}, u32[]{:S(2)}) copy-start(bf16[512,640]{1,0:T(8,128)(2,1)S(1)} %get-tuple-element.15) | copy-start | bytes 1966084
  83.4 2.3 copy-start.3
  85.7 0.7 copy-start.15
  85.7 43.2 %copy-start.16 = (s32[2]{0:T(128)S(1)}, s32[2]{0:T(128)}, u32[]{:S(2)}) copy-start(s32[2]{0:T(128)} %param.9) | copy-start | bytes 28
  85.7 45.9 %copy-start.17 = (u32[256]{0:T(256)S(1)}, u32[256]{0:T(256)}, u32[]{:S(2)}) copy-start(u32[256]{0:T(256)} %constant.139) | copy-start | bytes 3076
  85.7 41.5 %copy-start.8 = (bf16[2,64,1280]{2,1,0:T(8,128)(2,1)S(1)}, bf16[2,64,1280]{2,1,0:T(8,128)(2,1)}, u32[]{:S(2)}) copy-start(bf16[2,64,1280]{2,1,0:T(8,128)(2,1)} %param.7) | copy-start | bytes 983044
  85.8 81.3 %all-gather.6.cloned.1.call-start = ((), (), s32[]{:S(2)}) async-start(), calls=%async_computation.5 | async-start | bytes 1474560 | tf_op jit(solution)/shard_map/all_gather | solution.py:30
  128.9 147.3 %reduce-scatter.13.cloned.1.call-start = ((), (), s32[]{:S(2)}) async-start(), calls=%async_computation.6 | async-start | bytes 1474560 | tf_op jit(solution)/shard_map/reduce_scatter | solution.py:34
  167.1 1.8 copy-start.6
  205.9 25.8 %copy-start.7 = (f32[512,640]{1,0:T(8,128)S(1)}, f32[512,640]{1,0:T(8,128)}, u32[]{:S(2)}) copy-start(f32[512,640]{1,0:T(8,128)} %get-tuple-element.18) | copy-start | bytes 3932164
  231.7 1.4 copy-start.13
  236.9 39.2 %copy-start.1 = (bf16[64,1280]{1,0:T(8,128)(2,1)S(1)}, bf16[64,1280]{1,0:T(8,128)(2,1)}, u32[]{:S(2)}) copy-start(bf16[64,1280]{1,0:T(8,128)(2,1)} %get-tuple-element.12) | copy-start | bytes 491524
  236.9 80.4 %copy-start.19 = (bf16[512,640]{1,0:T(8,128)(2,1)S(1)}, bf16[512,640]{1,0:T(8,128)(2,1)}, u32[]{:S(2)}) copy-start(bf16[512,640]{1,0:T(8,128)(2,1)} %copy-done.18) | copy-start | bytes 1966084
  237.0 80.3 %all-gather.8.cloned.1.call-start = ((), (), s32[]{:S(2)}) async-start(), calls=%async_computation.7 | async-start | bytes 1474560 | tf_op jit(solution)/shard_map/all_gather | solution.py:30
  279.0 180.0 %reduce-scatter.17.cloned.1.call-start = ((), (), s32[]{:S(2)}) async-start(), calls=%async_computation.10 | async-start | bytes 1689600
  317.3 3.8 copy-start.10
  321.0 1.4 copy-start.4
  321.0 1.4 copy-start.12
  321.0 276.0 %reduce-scatter.15.cloned.1.call-start = ((), (), s32[]{:S(2)}) async-start(), calls=%async_computation.9 | async-start | bytes 1689600
Sparse Core Ops, SparseCore 0:
  9.8 41.3 all-gather.9
  85.9 41.2 reduce-scatter.10
  129.0 38.0 all-gather.5
  237.1 39.0 reduce-scatter.12
  279.1 38.1 all-gather.7
  321.2 137.7 reduce-scatter.16
  461.7 135.2 reduce-scatter.14

commit v2 on v1

v2 whole, which is shorter than its diff:
```python
import functools
import math

import jax
import jax.numpy as jnp
from jax import lax
from jax.experimental import pallas as pl
from jax.experimental.pallas import tpu as pltpu
from jax.sharding import PartitionSpec as P

STEPS = 50
EPS = 1e-06
MESH = pl.DeviceIdType.MESH
F32, BF16 = jnp.float32, jnp.bfloat16

ORDER = (4, 5, 3, 6, 2, 7, 1, 0)
POS = {slot: pos for pos, slot in enumerate(ORDER)}
NZ, NR = 8, 4


def gelu_and_slope(value):
    cdf = 0.5 * (1.0 + lax.erf(value * (1.0 / math.sqrt(2.0))))
    pdf = jnp.exp(-0.5 * value * value) * (1.0 / math.sqrt(2.0 * math.pi))
    return value * cdf, cdf + value * pdf


def nt(left, right):
    return lax.dot_general(left, right, (((1,), (1,)), ((), ())), preferred_element_type=F32)


def tn(left, right):
    return lax.dot_general(left, right, (((0,), (0,)), ((), ())), preferred_element_type=F32)


def kernel(
    lat, steps, ids, table, gains, win, wout, gin, gout,
    w_in, w_out, lats, xn0, h0, sl0, imgs, xn1, sl1, gh1, geps, gh0, hp, pf, pf2, stg1, rcv1, stg2,
    rcv2, idb, hm, pm, pmsg, prcv, acc, cstg, crcv, rstg, rrcv, tstg, tsum, trcv,
    local_sem, w_send, w_recv, ag_send, ag_recv, rs_send, rs_recv, id_send, id_recv, p_send, p_recv,
    c_send, c_recv, g_send, g_recv, t_send, t_recv,
):
    tok, width = lat.shape[1], lat.shape[2]
    half = tok // 2
    hidden = win.shape[2]
    sec, dp, me = lax.axis_index("sec"), lax.axis_index("dp"), lax.axis_index("tp")
    x, ylo, core = dp // 4, (dp // 2) % 2, dp % 2
    y = sec * 2 + ylo
    other = 1 - sec

    def at_z(distance):
        return {"tp": (me + distance + NZ) % NZ}

    def at_x(distance):
        return {"dp": ((x + distance + NR) % NR) * 4 + ylo * 2 + core}

    def at_y(distance):
        there = (y + distance + NR) % NR
        return {"sec": there // 2, "dp": x * 4 + (there % 2) * 2 + core}

    partner = {"dp": x * 4 + ylo * 2 + (1 - core)}
    across = {"sec": other, "dp": x * 4 + (1 - ylo) * 2 + core}
    pending = []

    def remote(src, dst, send_sem, recv_sem, device):
        return pltpu.make_async_remote_copy(
            src_ref=src, dst_ref=dst, send_sem=send_sem, recv_sem=recv_sem,
            device_id=device, device_id_type=MESH,
        )

    def go(copy):
        copy.start()
        pending.append(copy)

    here = [
        pltpu.make_async_copy(lat.at[sec], lats.at[pl.ds(POS[0] * tok, tok)], local_sem.at[0]),
        pltpu.make_async_copy(win.at[0], w_in.at[sec], local_sem.at[1]),
        pltpu.make_async_copy(wout.at[0], w_out.at[sec], local_sem.at[2]),
    ]
    for copy in here:
        copy.start()
    idb[0] = jnp.full((8, 128), ids[sec], jnp.int32)

    peers = [at_z(k) for k in range(1, NZ)] + [partner]
    peers += [at_x(k) for k in range(1, NR)] + [at_y(k) for k in range(1, NR)]
    barrier = pltpu.get_barrier_semaphore()
    for peer in peers:
        pl.semaphore_signal(barrier, inc=1, device_id=peer, device_id_type=MESH)
    pl.semaphore_wait(barrier, len(peers))

    def gather_copy(phase, buf, way, step, part):
        if way == 0:
            src, dst, device = POS[step - 1], POS[step], at_z(1)
        else:
            src, dst, device = POS[(NZ - step + 1) % NZ], POS[NZ - step], at_z(-1)
        at = (phase, way, 2 * (step - 1) + part)
        return remote(
            buf.at[pl.ds(src * tok + part * half, half)],
            buf.at[pl.ds(dst * tok + part * half, half)],
            ag_send.at[at], ag_recv.at[at], device,
        )

    def gather_begin(phase, buf, part):
        for way in (0, 1):
            go(gather_copy(phase, buf, way, 1, part))

    def gather_step(phase, buf, step):
        for part in (0, 1):
            for way in (0, 1):
                if step == NZ // 2 and part != way:
                    continue
                gather_copy(phase, buf, way, step, part).wait_recv()
                if step + 1 < NZ // 2 or (step + 1 == NZ // 2 and part == way):
                    go(gather_copy(phase, buf, way, step + 1, part))

    def arrived(step):
        if step == 0:
            return POS[0] * tok, tok
        if step == NZ // 2:
            return 0, tok
        return POS[NZ - step] * tok, 2 * tok

    def scatter_copy(phase, stg, rcv, way, step, part):
        at = (phase, way, 2 * (step - 1) + part)
        rows = pl.ds(part * half, half)
        return remote(
            stg.at[way, step - 1, rows], rcv.at[way, step - 1, rows],
            rs_send.at[at], rs_recv.at[at], at_z(1) if way == 0 else at_z(-1),
        )

    def scatter_step(phase, stg, rcv, step):
        rows = [(part, way) for part in (0, 1) for way in (0, 1)]
        if step == 1:
            rows = [(0, 0), (1, 1)]
        if step == 2:
            rows = [(1, 0), (0, 1), (0, 0), (1, 1)]
        for part, way in rows:
            at = pl.ds(part * half, half)
            base = part * half + (way * tok if step > 1 else 0)
            value = pf[pl.ds(base, half), :]
            if step > 2 or (step == 2 and part == way):
                scatter_copy(phase, stg, rcv, way, step - 1, part).wait_recv()
                value = value + rcv[way, step - 2, at, :].astype(F32)
            stg[way, step - 1, at, :] = value.astype(BF16)
            go(scatter_copy(phase, stg, rcv, way, step, part))

    def scatter_end(phase, stg, rcv, part):
        for way in (0, 1):
            scatter_copy(phase, stg, rcv, way, NZ // 2, part).wait_recv()

    def chunk(step):
        return arrived(5 - step) if step > 1 else (0, tok)

    def piece(quarter):
        return pl.ds(pl.multiple_of((quarter % 4) * 320 + core * 160, 32), 160)

    held = (w_in, w_out)
    given = (win, wout)

    def weight_copy(a, kind):
        if kind < 2:
            rows = piece(x + 2 * kind)
            src, dst, device = given[a].at[0, rows], held[a].at[sec, rows], across
        elif kind < 4:
            rows = piece(x)
            src = dst = held[a].at[other, rows]
            device = at_x(1) if kind == 2 else at_x(-1)
        else:
            rows = piece(x + (0, 2, 3, 1)[kind - 4])
            src = dst = held[a].at[other, rows]
            device = partner
        return remote(src, dst, w_send.at[a, kind], w_recv.at[a, kind], device)

    def weight_landed(a, kind):
        if kind < 4:
            rows = piece(x + (0, 2, 3, 1)[kind])
        else:
            quarter = (x + (0, 2, 3, 1)[kind - 4]) % 4
            rows = pl.ds(pl.multiple_of(quarter * 320 + (1 - core) * 160, 32), 160)
        ref = held[a].at[other, rows]
        remote(ref, ref, w_send.at[a, kind], w_recv.at[a, kind], partner).wait_recv()

    def weights_first(a):
        weight_landed(a, 0)
        go(weight_copy(a, 2))
        go(weight_copy(a, 3))
        go(weight_copy(a, 4))
        go(weight_copy(a, 1))

    def weights_second(a):
        for kind in (2, 3, 1):
            weight_landed(a, kind)
            go(weight_copy(a, {2: 6, 3: 7, 1: 5}[kind]))

    def weights_last(a):
        for kind in (4, 6, 7, 5):
            weight_landed(a, kind)

    def each(count, rows, body, init=None):
        return lax.fori_loop(0, count // rows, lambda i, c: body(pl.multiple_of(i * rows, rows), c), init)

    def norm(buf, dst, start, count, gain, slots=None):
        def body(at, total):
            value = buf[pl.ds(start + at, 16), :].astype(F32)
            scale = lax.rsqrt(jnp.mean(value * value, axis=-1, keepdims=True) + EPS)
            dst[pl.ds(start + at, 16), :] = (value * scale * gain).astype(BF16)
            return None if total is None else total + value[:8] + value[8:]

        if slots is None:
            each(count, 16, body)
            return
        for index, slot in enumerate(slots):
            start = POS[slot] * tok
            total = each(tok, 16, body, jnp.zeros((8, width), F32))
            pm[pl.ds(slot, 1), :] = jnp.sum(total, axis=0, keepdims=True) * (1.0 / tok)

    def slots_of(start, count):
        return ORDER[start // tok:(start + count) // tok]

    theta = (jnp.full((1, 128), steps[sec], jnp.int32).astype(F32) + 1.0) * (
        math.pi / 2.0 / (STEPS + 1.0)
    )
    alpha, sigma = jnp.cos(theta)[:, :1], jnp.sin(theta)[:, :1]
    go(weight_copy(0, 0))
    here[0].wait()
    for part in (0, 1):
        gather_begin(0, lats, part)
    for k in range(1, NZ):
        go(remote(idb.at[0], idb.at[k], id_send.at[k - 1], id_recv.at[k - 1], at_z(k)))
    gain0, gain1 = gains[0:1, :], gains[1:2, :]
    norm(lats, xn0, *arrived(0), gain0)
    gather_step(0, lats, 1)
    weights_first(0)
    norm(lats, xn0, *arrived(1), gain0)
    gather_step(0, lats, 2)
    weights_second(0)
    go(weight_copy(1, 0))
    norm(lats, xn0, *arrived(2), gain0)
    gather_step(0, lats, 3)
    norm(lats, xn0, *arrived(3), gain0)
    gather_step(0, lats, 4)
    norm(lats, xn0, *arrived(4), gain0)
    weights_last(0)
    weights_first(1)
    here[1].wait()

    def hidden0(start, count):
        hp[pl.ds(0, count), :] = jnp.dot(
            xn0[pl.ds(start, count), :], w_in[0], preferred_element_type=F32
        )

        def body(at, carry):
            act, slope = gelu_and_slope(hp[pl.ds(at, 16), :])
            h0[pl.ds(start + at, 16), :] = act.astype(BF16)
            sl0[pl.ds(start + at, 16), :] = slope
            return carry

        each(count, 16, body)

    for step in range(1, 6):
        hidden0(*chunk(step))
        if step == 1:
            weights_second(1)
    weights_last(1)
    here[2].wait()

    for step in range(1, 6):
        start, count = chunk(step)
        out = nt(h0[pl.ds(start, count), :], w_out[0])
        if step < 5:
            pf[pl.ds(0, count), :] = out
            scatter_step(0, stg1, rcv1, step)
        else:
            pf2[...] = out

    own = POS[0] * tok
    for part in (0, 1):
        scatter_end(0, stg1, rcv1, part)

        def images(at, carry):
            rows = pl.ds(part * half + at, 16)
            base = lats[pl.ds(own + part * half + at, 16), :].astype(F32)
            mix = pf2[rows, :] + (rcv1[0, 3, rows, :].astype(F32) + rcv1[1, 3, rows, :].astype(F32))
            imgs[pl.ds(own + part * half + at, 16), :] = (
                (base - sigma * (base + mix)) / alpha
            ).astype(BF16)
            return carry

        each(half, 16, images)
        gather_begin(1, imgs, part)

    def hidden1(start, count):
        slots = slots_of(start, count)
        norm(imgs, xn1, start, count, gain1, slots)
        hp[pl.ds(0, count), :] = jnp.dot(
            xn1[pl.ds(start, count), :], w_in[1], preferred_element_type=F32
        )
        for index, slot in enumerate(slots):
            def body(at, total):
                act, slope = gelu_and_slope(hp[pl.ds(index * tok + at, 16), :])
                sl1[pl.ds(start + index * tok + at, 16), :] = slope
                act = act.astype(BF16).astype(F32)
                return total + act[:8] + act[8:]

            total = each(tok, 16, body, jnp.zeros((8, hidden), F32))
            hm[pl.ds(slot, 1), :] = jnp.sum(total, axis=0, keepdims=True) * (1.0 / tok)

    hidden1(*arrived(0))
    for k in range(1, NZ):
        remote(idb.at[k], idb.at[k], id_send.at[k - 1], id_recv.at[k - 1], at_z(k)).wait_recv()
    id_rows = jnp.concatenate([idb[k, 0:1, :] for k in range(NZ)], axis=0)
    prompts = table.shape[0]
    onehot = (
        id_rows[:, :prompts] == lax.broadcasted_iota(jnp.int32, (NZ, prompts), 1)
    ).astype(F32).astype(BF16)
    text = jnp.dot(onehot, table[...], preferred_element_type=F32)
    text = text * lax.rsqrt(jnp.mean(text * text, axis=-1, keepdims=True) + EPS)
    for step in range(1, 5):
        gather_step(1, imgs, step)
        hidden1(*arrived(step))

    mean1 = hm[...]
    high = mean1.astype(BF16).astype(F32)
    both = jnp.concatenate([high, mean1 - high], axis=0).astype(BF16)
    mixed = nt(both, w_out[1])
    mixed = mixed[:NZ] + mixed[NZ:]
    mid = width // 2
    pmsg[...] = jnp.concatenate([mixed[:, :mid], mixed[:, mid:]], axis=0).astype(BF16)
    for k in range(1, NZ):
        go(remote(pmsg, prcv.at[k - 1], p_send.at[k - 1], p_recv.at[k - 1], at_z(k)))
    pooled = pm[...] + mixed
    for k in range(1, NZ):
        remote(pmsg, prcv.at[k - 1], p_send.at[k - 1], p_recv.at[k - 1], at_z(k)).wait_recv()
        got = prcv[k - 1].astype(F32)
        got = jnp.concatenate([got[:NZ], got[NZ:]], axis=1)
        pooled = pooled + jnp.concatenate([got[NZ - k:], got[:NZ - k]], axis=0)
    unit = lax.rsqrt(jnp.mean(pooled * pooled, axis=-1, keepdims=True) + EPS)
    g_mean = (unit * text - pooled * (unit * unit * unit) * jnp.mean(
        pooled * text, axis=-1, keepdims=True
    )) * (-100.0 / width / tok)
    g_h1 = jnp.dot(g_mean.astype(BF16), w_out[1], preferred_element_type=F32)
    g_own = g_mean[0:1, :]

    for step in range(1, 6):
        start, count = chunk(step)
        for index, slot in enumerate(slots_of(start, count)):
            row = g_h1[slot:slot + 1, :]

            def slope_times(at, carry):
                rows = pl.ds(start + index * tok + at, 16)
                gh1[rows, :] = (row * sl1[rows, :]).astype(BF16)
                return carry

            each(tok, 16, slope_times)
        out = nt(gh1[pl.ds(start, count), :], w_in[1])
        if step < 5:
            pf[pl.ds(0, count), :] = out
            scatter_step(1, stg2, rcv2, step)
        else:
            pf2[...] = out

    ratio = -(sigma / alpha)
    for part in (0, 1):
        scatter_end(1, stg2, rcv2, part)

        def back(at, carry):
            rows = pl.ds(part * half + at, 16)
            seen = imgs[pl.ds(own + part * half + at, 16), :].astype(F32)
            g_xn = pf2[rows, :] + (
                rcv2[0, 3, rows, :].astype(F32) + rcv2[1, 3, rows, :].astype(F32)
            )
            scale = lax.rsqrt(jnp.mean(seen * seen, axis=-1, keepdims=True) + EPS)
            weighted = gain1 * g_xn
            g_norm = scale * weighted - seen * (scale * scale * scale) * jnp.mean(
                seen * weighted, axis=-1, keepdims=True
            )
            g_images = (g_own + g_norm).astype(BF16).astype(F32)
            geps[pl.ds(own + part * half + at, 16), :] = (ratio * g_images).astype(BF16)
            return carry

        each(half, 16, back)
        gather_begin(2, geps, part)

    def hidden_back(start, count):
        hp[pl.ds(0, count), :] = jnp.dot(
            geps[pl.ds(start, count), :], w_out[0], preferred_element_type=F32
        )

        def body(at, carry):
            rows = pl.ds(start + at, 16)
            gh0[rows, :] = (hp[pl.ds(at, 16), :] * sl0[rows, :]).astype(BF16)
            return carry

        each(count, 16, body)

    def weight_terms(start, count, first):
        rows = pl.ds(start, count)
        for a, (left, right) in enumerate(((geps, h0), (xn0, gh0))):
            def body(i, carry):
                cols = pl.ds(pl.multiple_of(i * 256, 256), 256)
                term = tn(left[rows, cols], right[rows, :])
                if first:
                    acc[a, cols, :] = term
                else:
                    acc[a, cols, :] += term
                return carry

            lax.fori_loop(0, width // 256, body, None)

    hidden_back(*arrived(0))
    for step in range(1, 5):
        gather_step(2, geps, step)
        hidden_back(*arrived(step))
        if step == 2:
            weight_terms(4 * tok, 4 * tok, True)
    weight_terms(0, 4 * tok, False)

    def rows_of(a, slab, j, which):
        cx, cy = (slab, j) if a == 0 else (j, slab)
        return pl.ds(pl.multiple_of((cy // 2) * 640 + cx * 160 + (cy % 2) * 80 + which * 40, 40), 40)

    def pair(a, slab, part, which):
        return jnp.concatenate(
            [acc[a, rows_of(a, slab, 2 * part + j, which), :] for j in (0, 1)], axis=0
        )

    place = (x, y)
    along = (at_x, at_y)

    def core_copy(a, n):
        slab = (place[a] + (2, 1, 3, 0)[n]) % NR
        return remote(cstg.at[a, slab], crcv.at[a, slab], c_send.at[a, n], c_recv.at[a, n], partner)

    for n in range(4):
        for a in (0, 1):
            slab = (place[a] + (2, 1, 3, 0)[n]) % NR
            for part in (0, 1):
                cstg[a, slab, pl.ds(80 * part, 80), :] = pair(a, slab, part, 1 - core).astype(BF16)
            go(core_copy(a, n))

    def own_part(a, distance, part):
        slab = (place[a] + distance) % NR
        return pair(a, slab, part, core) + crcv[a, slab, pl.ds(80 * part, 80), :].astype(F32)

    def ring_copy(a, way, step, part):
        at = (a, way, 2 * (step - 1) + part)
        rows = pl.ds(80 * part, 80)
        return remote(
            rstg.at[a, way, step - 1, rows], rrcv.at[a, way, step - 1, rows],
            g_send.at[at], g_recv.at[at], along[a](1 if way == 0 else -1),
        )

    for a in (0, 1):
        core_copy(a, 0).wait_recv()
        for way in (0, 1):
            rstg[a, way, 0, pl.ds(80 * way, 80), :] = own_part(a, 2, way).astype(BF16)
            go(ring_copy(a, way, 1, way))
    for a in (0, 1):
        for way in (0, 1):
            core_copy(a, 1 + way).wait_recv()
            for part in (1 - way, way):
                value = own_part(a, 1 if way == 0 else 3, part)
                if part == way:
                    ring_copy(a, way, 1, part).wait_recv()
                    value = value + rrcv[a, way, 0, pl.ds(80 * part, 80), :].astype(F32)
                rstg[a, way, 1, pl.ds(80 * part, 80), :] = value.astype(BF16)
                go(ring_copy(a, way, 2, part))

    def last_copy(a, k):
        target = (place[1 - a] + k) % NR
        return remote(
            tstg.at[a, target], trcv.at[a, k - 1], t_send.at[a, k - 1], t_recv.at[a, k - 1],
            along[1 - a](k),
        )

    for a in (0, 1):
        core_copy(a, 3).wait_recv()
        for part in (0, 1):
            value = own_part(a, 0, part)
            for way in (0, 1):
                ring_copy(a, way, 2, part).wait_recv()
                value = value + rrcv[a, way, 1, pl.ds(80 * part, 80), :].astype(F32)
            for j in (0, 1):
                rows = value[40 * j:40 * j + 40]
                tsum[a, 2 * part + j] = rows
                tstg[a, 2 * part + j] = jnp.concatenate(
                    [rows, jnp.zeros((8, hidden), F32)], axis=0
                ).astype(BF16)
        for k in range(1, NR):
            go(last_copy(a, k))
    for a, result in enumerate((gout, gin)):
        total = tsum[a, place[1 - a]]
        for k in range(1, NR):
            last_copy(a, k).wait_recv()
            total = total + trcv[a, k - 1].astype(F32)[:40]
        result[...] = total
    for copy in pending:
        copy.wait_send()


def on_device(latents, timesteps, prompt_ids, prompt_table, gains, w_in, w_out):
    tok, width = latents.shape[1:]
    hidden = w_in.shape[2]
    rows = NZ * tok
    vmem, dma = pltpu.VMEM, pltpu.SemaphoreType.DMA
    scratch = [
        vmem((2, width, hidden), BF16),
        vmem((2, width, hidden), BF16),
        vmem((rows, width), BF16),
        vmem((rows, width), BF16),
        vmem((rows, hidden), BF16),
        vmem((rows, hidden), F32),
        vmem((rows, width), BF16),
        vmem((rows, width), BF16),
        vmem((rows, hidden), F32),
        vmem((rows, hidden), BF16),
        vmem((rows, width), BF16),
        vmem((rows, hidden), BF16),
        vmem((2 * tok, hidden), F32),
        vmem((2 * tok, width), F32),
        vmem((tok, width), F32),
        vmem((2, 4, tok, width), BF16),
        vmem((2, 4, tok, width), BF16),
        vmem((2, 4, tok, width), BF16),
        vmem((2, 4, tok, width), BF16),
        vmem((NZ, 8, 128), jnp.int32),
        vmem((NZ, hidden), F32),
        vmem((NZ, width), F32),
        vmem((2 * NZ, width // 2), BF16),
        vmem((NZ - 1, 2 * NZ, width // 2), BF16),
        vmem((2, width, hidden), F32),
        vmem((2, NR, 160, hidden), BF16),
        vmem((2, NR, 160, hidden), BF16),
        vmem((2, 2, 2, 160, hidden), BF16),
        vmem((2, 2, 2, 160, hidden), BF16),
        vmem((2, NR, 48, hidden), BF16),
        vmem((2, NR, 40, hidden), F32),
        vmem((2, NR - 1, 48, hidden), BF16),
        dma((3,)),
        dma((2, 8)), dma((2, 8)),
        dma((3, 2, 8)), dma((3, 2, 8)),
        dma((2, 2, 8)), dma((2, 2, 8)),
        dma((7,)), dma((7,)),
        dma((7,)), dma((7,)),
        dma((2, 4)), dma((2, 4)),
        dma((2, 2, 4)), dma((2, 2, 4)),
        dma((2, 3)), dma((2, 3)),
    ]
    whole, scalar, away = (pl.BlockSpec(memory_space=s) for s in (pltpu.VMEM, pltpu.SMEM, pl.ANY))
    share = jax.ShapeDtypeStruct((width // 32, hidden), F32)
    return pl.pallas_call(
        kernel,
        out_shape=(share, share),
        in_specs=[away, scalar, scalar, whole, whole, away, away],
        out_specs=(whole, whole),
        scratch_shapes=scratch,
        compiler_params=pltpu.CompilerParams(
            collective_id=0, has_side_effects=True, vmem_limit_bytes=56 * 2**20
        ),
        name="draft_step",
    )(latents, timesteps, prompt_ids, prompt_table, gains, w_in, w_out)


def solution(mesh):
    in_specs = (
        P(("dp", "tp"), None, None),
        P(("dp", "tp")),
        P(("dp", "tp")),
        P(),
        P(),
        P("sec", None, "tp"),
        P("sec", None, "tp"),
    )
    out_specs = (P(("sec", "dp"), "tp"), P(("sec", "dp"), "tp"))
    return jax.shard_map(
        on_device, mesh=mesh, in_specs=in_specs, out_specs=out_specs, check_vma=False
    )
```

time: 606 us -> 147 us (0.24)
  waiting for transfers between devices: 478 us -> 0 us
  Pallas kernels: 0 us -> 142 us
  blocking collectives: 51.8 us -> 0 us
  matrix products: 31 us -> 0 us
  between operations: 17.3 us -> 0.64 us
  other arithmetic: 15 us -> 0 us
    unnamed x9 -> x0, waiting for transfers between devices: 267 us -> none
    pallas_call x0 -> x1, Pallas kernels: none -> 142 us  [on_device(): pl.pallas_call(kernel, out_shape=(share, share), in_specs=[away, scalar,...]
    all_gather x3 -> x0, waiting for transfers between devices: 109 us -> none  [collect(): return lax.all_gather(piece, 'tp', axis=0, tiled=True)]
    reduce_scatter x2 -> x0, waiting for transfers between devices: 78.5 us -> none  [reduce_rows(): lax.psum_scatter(value, 'tp', scatter_dimension=0, tiled=True)]
    dot_general x10 -> x0, matrix products: 31 us -> none  [the longest x2 9.55 us: contract_first(): lax.dot_general(left, right, (((0,), (0,)), ((), ())), preferred_element_...]
    unnamed x1 -> x0, blocking collectives: 27.2 us -> none
    all_gather x1 -> x0, blocking collectives: 24.6 us -> none  [collect(): return lax.all_gather(piece, 'tp', axis=0, tiled=True)]
    ppermute x2 -> x0, waiting for transfers between devices: 22.8 us -> none  [the longest x1 22.8 us: on_device(): other_out = lax.ppermute(w_out[0], 'sec', swap)]
  transfers between devices with their start and end apart: 9 -> 0, of which waited for: 8 -> 0; matrix products, arithmetic and copies ran while one was open for 3% -> 0% of each run, Pallas kernels for 0% -> 0%
where the time goes in v2:
time: 147 us; the launch traced here: 146 us
  Pallas kernels  142 us (97%)
  local copies, waits for them, and re-layouts  3.09 us (2%)
    pallas_call x1, Pallas kernels, on_device(): pl.pallas_call(kernel, out_shape=(share, share), in_specs=[away, scalar,...  142 us
    unnamed x2, local copies, waits for them, and re-layouts  3.09 us

profile of v2, /device:TPU:32, one launch (start us, length us, event | category | flops | bytes accessed | tf_op | source)
XLA Modules:
  0.0 145.5 jit_solution(3468182800673110949)
XLA Ops:
  0.6 141.8 %draft_step.1 = (f32[40,640]{1,0:T(8,128)}, f32[40,640]{1,0:T(8,128)}) custom-call(bf16[2,64,1280]{2,1,0:T(8,128)(2,1)} %lat.1, s32[2]{0:T(128)} %steps.1, s32[2]{0:T(128)} %ids.1, bf16[64,1280]{1,0:T(8,128)(2,1)} %table.1, f32[2,1280]{1,0:T(2,128)} %gains.1, bf16[1,1280,640]{2,1,0:T(8,128)(2,1)} %win.1, bf16[1,1280,640]{2,1,0:T(8,128)(2,1)} %wout.1), custom_call_target="tpu_custom_call" | custom-call | tf_op jit(solution)/shard_map/draft_step/pallas_call | solution.py:550
  142.4 1.5 %copy.11 = f32[40,640]{1,0:T(8,128)} copy(f32[40,640]{1,0:T(8,128)} %get-tuple-element.4) | data formatting | bytes 204800
  144.0 1.5 %copy.12 = f32[40,640]{1,0:T(8,128)} copy(f32[40,640]{1,0:T(8,128)} %get-tuple-element.5) | data formatting | bytes 204800

commit v3 on v2

--- a/solution.py
+++ b/solution.py
@@ -16,6 +16,7 @@
 ORDER = (4, 5, 3, 6, 2, 7, 1, 0)
 POS = {slot: pos for pos, slot in enumerate(ORDER)}
 NZ, NR = 8, 4
+PARTS = 4
 
 
 def gelu_and_slope(value):
@@ -40,7 +41,7 @@
     c_send, c_recv, g_send, g_recv, t_send, t_recv,
 ):
     tok, width = lat.shape[1], lat.shape[2]
-    half = tok // 2
+    size = tok // PARTS
     hidden = win.shape[2]
     sec, dp, me = lax.axis_index("sec"), lax.axis_index("dp"), lax.axis_index("tp")
     x, ylo, core = dp // 4, (dp // 2) % 2, dp % 2
@@ -59,7 +60,6 @@
 
     partner = {"dp": x * 4 + ylo * 2 + (1 - core)}
     across = {"sec": other, "dp": x * 4 + (1 - ylo) * 2 + core}
-    pending = []
 
     def remote(src, dst, send_sem, recv_sem, device):
         return pltpu.make_async_remote_copy(
@@ -67,9 +67,8 @@
             device_id=device, device_id_type=MESH,
         )
 
-    def go(copy):
-        copy.start()
-        pending.append(copy)
+    def sent(ref, send_sem):
+        remote(ref, ref, send_sem, c_recv.at[0, 0], partner).wait_send()
 
     here = [
         pltpu.make_async_copy(lat.at[sec], lats.at[pl.ds(POS[0] * tok, tok)], local_sem.at[0]),
@@ -87,30 +86,35 @@
         pl.semaphore_signal(barrier, inc=1, device_id=peer, device_id_type=MESH)
     pl.semaphore_wait(barrier, len(peers))
 
-    def gather_copy(phase, buf, way, step, part):
+    def far(part, way):
+        return part // (PARTS // 2) == way
+
+    def parts_of(farthest):
+        if farthest:
+            return [(p + way * (PARTS // 2), way) for p in range(PARTS // 2) for way in (0, 1)]
+        return [(part, way) for part in range(PARTS) for way in (0, 1)]
+
+    def gather_copy(buf, way, step, part):
         if way == 0:
             src, dst, device = POS[step - 1], POS[step], at_z(1)
         else:
             src, dst, device = POS[(NZ - step + 1) % NZ], POS[NZ - step], at_z(-1)
-        at = (phase, way, 2 * (step - 1) + part)
+        at = (way, PARTS * (step - 1) + part)
         return remote(
-            buf.at[pl.ds(src * tok + part * half, half)],
-            buf.at[pl.ds(dst * tok + part * half, half)],
-            ag_send.at[at], ag_recv.at[at], device,
-        )
-
-    def gather_begin(phase, buf, part):
+            buf.at[pl.ds(src * tok + part * size, size)],
+            buf.at[pl.ds(dst * tok + part * size, size)],
+            ag_send, ag_recv.at[at], device,
+        )
+
+    def gather_begin(buf, part):
         for way in (0, 1):
-            go(gather_copy(phase, buf, way, 1, part))
-
-    def gather_step(phase, buf, step):
-        for part in (0, 1):
-            for way in (0, 1):
-                if step == NZ // 2 and part != way:
-                    continue
-                gather_copy(phase, buf, way, step, part).wait_recv()
-                if step + 1 < NZ // 2 or (step + 1 == NZ // 2 and part == way):
-                    go(gather_copy(phase, buf, way, step + 1, part))
+            gather_copy(buf, way, 1, part).start()
+
+    def gather_step(buf, step):
+        for part, way in parts_of(step == NZ // 2):
+            gather_copy(buf, way, step, part).wait_recv()
+            if step + 1 < NZ // 2 or (step + 1 == NZ // 2 and far(part, way)):
+                gather_copy(buf, way, step + 1, part).start()
 
     def arrived(step):
         if step == 0:
@@ -119,80 +123,71 @@
             return 0, tok
         return POS[NZ - step] * tok, 2 * tok
 
-    def scatter_copy(phase, stg, rcv, way, step, part):
-        at = (phase, way, 2 * (step - 1) + part)
-        rows = pl.ds(part * half, half)
+    def scatter_copy(stg, rcv, way, step, part):
+        at = (way, PARTS * (step - 1) + part)
+        rows = pl.ds(part * size, size)
         return remote(
             stg.at[way, step - 1, rows], rcv.at[way, step - 1, rows],
-            rs_send.at[at], rs_recv.at[at], at_z(1) if way == 0 else at_z(-1),
-        )
-
-    def scatter_step(phase, stg, rcv, step):
-        rows = [(part, way) for part in (0, 1) for way in (0, 1)]
-        if step == 1:
-            rows = [(0, 0), (1, 1)]
+            rs_send, rs_recv.at[at], at_z(1) if way == 0 else at_z(-1),
+        )
+
+    def scatter_step(stg, rcv, step):
+        rows = parts_of(step == 1)
         if step == 2:
-            rows = [(1, 0), (0, 1), (0, 0), (1, 1)]
+            rows.sort(key=lambda row: far(*row))
         for part, way in rows:
-            at = pl.ds(part * half, half)
-            base = part * half + (way * tok if step > 1 else 0)
-            value = pf[pl.ds(base, half), :]
-            if step > 2 or (step == 2 and part == way):
-                scatter_copy(phase, stg, rcv, way, step - 1, part).wait_recv()
+            at = pl.ds(part * size, size)
+            base = part * size + (way * tok if step > 1 else 0)
+            value = pf[pl.ds(base, size), :]
+            if step > 2 or (step == 2 and far(part, way)):
+                scatter_copy(stg, rcv, way, step - 1, part).wait_recv()
                 value = value + rcv[way, step - 2, at, :].astype(F32)
             stg[way, step - 1, at, :] = value.astype(BF16)
-            go(scatter_copy(phase, stg, rcv, way, step, part))
-
-    def scatter_end(phase, stg, rcv, part):
+            scatter_copy(stg, rcv, way, step, part).start()
+
+    def scatter_end(stg, rcv, part):
         for way in (0, 1):
-            scatter_copy(phase, stg, rcv, way, NZ // 2, part).wait_recv()
+            scatter_copy(stg, rcv, way, NZ // 2, part).wait_recv()
 
     def chunk(step):
         return arrived(5 - step) if step > 1 else (0, tok)
 
-    def piece(quarter):
-        return pl.ds(pl.multiple_of((quarter % 4) * 320 + core * 160, 32), 160)
+    quarter = (x + 2 * ylo) % NR
+
+    def piece(offset, which):
+        rows = (quarter + offset) % NR * (width // NR) + which * (width // NR // 2)
+        return pl.ds(pl.multiple_of(rows, 32), width // NR // 2)
 
     held = (w_in, w_out)
     given = (win, wout)
+    beside = {"dp": x * 4 + (1 - ylo) * 2 + core}
 
     def weight_copy(a, kind):
-        if kind < 2:
-            rows = piece(x + 2 * kind)
+        if kind == 0:
+            rows = piece(2, core)
             src, dst, device = given[a].at[0, rows], held[a].at[sec, rows], across
-        elif kind < 4:
-            rows = piece(x)
+        else:
+            rows = piece((0, 0, 0, 0, 0, 3, 1, 2)[kind], core)
             src = dst = held[a].at[other, rows]
-            device = at_x(1) if kind == 2 else at_x(-1)
-        else:
-            rows = piece(x + (0, 2, 3, 1)[kind - 4])
-            src = dst = held[a].at[other, rows]
-            device = partner
-        return remote(src, dst, w_send.at[a, kind], w_recv.at[a, kind], device)
+            device = (at_x(1), at_x(-1), beside, partner)[min(kind, 4) - 1]
+        return remote(src, dst, w_send, w_recv.at[a, kind], device)
 
     def weight_landed(a, kind):
-        if kind < 4:
-            rows = piece(x + (0, 2, 3, 1)[kind])
-        else:
-            quarter = (x + (0, 2, 3, 1)[kind - 4]) % 4
-            rows = pl.ds(pl.multiple_of(quarter * 320 + (1 - core) * 160, 32), 160)
-        ref = held[a].at[other, rows]
-        remote(ref, ref, w_send.at[a, kind], w_recv.at[a, kind], partner).wait_recv()
+        ref = held[a].at[other, piece((0, 3, 1, 2)[kind % 4], core if kind < 4 else 1 - core)]
+        remote(ref, ref, w_send, w_recv.at[a, kind], partner).wait_recv()
 
     def weights_first(a):
         weight_landed(a, 0)
-        go(weight_copy(a, 2))
-        go(weight_copy(a, 3))
-        go(weight_copy(a, 4))
-        go(weight_copy(a, 1))
+        for kind in (1, 2, 3, 4):
+            weight_copy(a, kind).start()
 
     def weights_second(a):
-        for kind in (2, 3, 1):
+        for kind in (1, 2, 3):
             weight_landed(a, kind)
-            go(weight_copy(a, {2: 6, 3: 7, 1: 5}[kind]))
+            weight_copy(a, kind + 4).start()
 
     def weights_last(a):
-        for kind in (4, 6, 7, 5):
+        for kind in (4, 5, 6, 7):
             weight_landed(a, kind)
 
     def each(count, rows, body, init=None):
@@ -220,28 +215,28 @@
         math.pi / 2.0 / (STEPS + 1.0)
     )
     alpha, sigma = jnp.cos(theta)[:, :1], jnp.sin(theta)[:, :1]
-    go(weight_copy(0, 0))
+    weight_copy(0, 0).start()
+    weight_copy(1, 0).start()
     here[0].wait()
-    for part in (0, 1):
-        gather_begin(0, lats, part)
+    for part in range(PARTS):
+        gather_begin(lats, part)
     for k in range(1, NZ):
-        go(remote(idb.at[0], idb.at[k], id_send.at[k - 1], id_recv.at[k - 1], at_z(k)))
+        remote(idb.at[0], idb.at[k], id_send, id_recv.at[k - 1], at_z(k)).start()
     gain0, gain1 = gains[0:1, :], gains[1:2, :]
     norm(lats, xn0, *arrived(0), gain0)
-    gather_step(0, lats, 1)
+    gather_step(lats, 1)
     weights_first(0)
     norm(lats, xn0, *arrived(1), gain0)
-    gather_step(0, lats, 2)
+    gather_step(lats, 2)
+    norm(lats, xn0, *arrived(2), gain0)
+    weights_first(1)
+    gather_step(lats, 3)
     weights_second(0)
-    go(weight_copy(1, 0))
-    norm(lats, xn0, *arrived(2), gain0)
-    gather_step(0, lats, 3)
     norm(lats, xn0, *arrived(3), gain0)
-    gather_step(0, lats, 4)
+    gather_step(lats, 4)
     norm(lats, xn0, *arrived(4), gain0)
+    here[1].wait()
     weights_last(0)
-    weights_first(1)
-    here[1].wait()
 
     def hidden0(start, count):
         hp[pl.ds(0, count), :] = jnp.dot(
@@ -256,37 +251,39 @@
 
         each(count, 16, body)
 
-    for step in range(1, 6):
-        hidden0(*chunk(step))
-        if step == 1:
-            weights_second(1)
+    hidden0(*chunk(1))
+    weights_second(1)
+    hidden0(*chunk(2))
+    here[2].wait()
     weights_last(1)
-    here[2].wait()
 
     for step in range(1, 6):
         start, count = chunk(step)
+        if step > 2:
+            hidden0(start, count)
         out = nt(h0[pl.ds(start, count), :], w_out[0])
         if step < 5:
             pf[pl.ds(0, count), :] = out
-            scatter_step(0, stg1, rcv1, step)
+            scatter_step(stg1, rcv1, step)
         else:
             pf2[...] = out
 
     own = POS[0] * tok
-    for part in (0, 1):
-        scatter_end(0, stg1, rcv1, part)
+    sent(lats.at[pl.ds(0, (NZ - 1) * tok)], ag_send)
+    for part in range(PARTS):
+        scatter_end(stg1, rcv1, part)
 
         def images(at, carry):
-            rows = pl.ds(part * half + at, 16)
-            base = lats[pl.ds(own + part * half + at, 16), :].astype(F32)
+            rows = pl.ds(part * size + at, 16)
+            base = lats[pl.ds(own + part * size + at, 16), :].astype(F32)
             mix = pf2[rows, :] + (rcv1[0, 3, rows, :].astype(F32) + rcv1[1, 3, rows, :].astype(F32))
-            imgs[pl.ds(own + part * half + at, 16), :] = (
+            imgs[pl.ds(own + part * size + at, 16), :] = (
                 (base - sigma * (base + mix)) / alpha
             ).astype(BF16)
             return carry
 
-        each(half, 16, images)
-        gather_begin(1, imgs, part)
+        each(size, 16, images)
+        gather_begin(imgs, part)
 
     def hidden1(start, count):
         slots = slots_of(start, count)
@@ -306,7 +303,7 @@
 
     hidden1(*arrived(0))
     for k in range(1, NZ):
-        remote(idb.at[k], idb.at[k], id_send.at[k - 1], id_recv.at[k - 1], at_z(k)).wait_recv()
+        remote(idb.at[k], idb.at[k], id_send, id_recv.at[k - 1], at_z(k)).wait_recv()
     id_rows = jnp.concatenate([idb[k, 0:1, :] for k in range(NZ)], axis=0)
     prompts = table.shape[0]
     onehot = (
@@ -315,7 +312,7 @@
     text = jnp.dot(onehot, table[...], preferred_element_type=F32)
     text = text * lax.rsqrt(jnp.mean(text * text, axis=-1, keepdims=True) + EPS)
     for step in range(1, 5):
-        gather_step(1, imgs, step)
+        gather_step(imgs, step)
         hidden1(*arrived(step))
 
     mean1 = hm[...]
@@ -326,10 +323,10 @@
     mid = width // 2
     pmsg[...] = jnp.concatenate([mixed[:, :mid], mixed[:, mid:]], axis=0).astype(BF16)
     for k in range(1, NZ):
-        go(remote(pmsg, prcv.at[k - 1], p_send.at[k - 1], p_recv.at[k - 1], at_z(k)))
+        remote(pmsg, prcv.at[k - 1], p_send, p_recv.at[k - 1], at_z(k)).start()
     pooled = pm[...] + mixed
     for k in range(1, NZ):
-        remote(pmsg, prcv.at[k - 1], p_send.at[k - 1], p_recv.at[k - 1], at_z(k)).wait_recv()
+        remote(pmsg, prcv.at[k - 1], p_send, p_recv.at[k - 1], at_z(k)).wait_recv()
         got = prcv[k - 1].astype(F32)
         got = jnp.concatenate([got[:NZ], got[NZ:]], axis=1)
         pooled = pooled + jnp.concatenate([got[NZ - k:], got[:NZ - k]], axis=0)
@@ -339,6 +336,7 @@
     )) * (-100.0 / width / tok)
     g_h1 = jnp.dot(g_mean.astype(BF16), w_out[1], preferred_element_type=F32)
     g_own = g_mean[0:1, :]
+    sent(lats.at[pl.ds(0, (NZ - 1) * tok)], rs_send)
 
     for step in range(1, 6):
         start, count = chunk(step)
@@ -354,17 +352,18 @@
         out = nt(gh1[pl.ds(start, count), :], w_in[1])
         if step < 5:
             pf[pl.ds(0, count), :] = out
-            scatter_step(1, stg2, rcv2, step)
+            scatter_step(stg2, rcv2, step)
         else:
             pf2[...] = out
 
     ratio = -(sigma / alpha)
-    for part in (0, 1):
-        scatter_end(1, stg2, rcv2, part)
+    sent(lats.at[pl.ds(0, (NZ - 1) * tok)], ag_send)
+    for part in range(PARTS):
+        scatter_end(stg2, rcv2, part)
 
         def back(at, carry):
-            rows = pl.ds(part * half + at, 16)
-            seen = imgs[pl.ds(own + part * half + at, 16), :].astype(F32)
+            rows = pl.ds(part * size + at, 16)
+            seen = imgs[pl.ds(own + part * size + at, 16), :].astype(F32)
             g_xn = pf2[rows, :] + (
                 rcv2[0, 3, rows, :].astype(F32) + rcv2[1, 3, rows, :].astype(F32)
             )
@@ -374,11 +373,11 @@
                 seen * weighted, axis=-1, keepdims=True
             )
             g_images = (g_own + g_norm).astype(BF16).astype(F32)
-            geps[pl.ds(own + part * half + at, 16), :] = (ratio * g_images).astype(BF16)
+            geps[pl.ds(own + part * size + at, 16), :] = (ratio * g_images).astype(BF16)
             return carry
 
-        each(half, 16, back)
-        gather_begin(2, geps, part)
+        each(size, 16, back)
+        gather_begin(geps, part)
 
     def hidden_back(start, count):
         hp[pl.ds(0, count), :] = jnp.dot(
@@ -392,27 +391,20 @@
 
         each(count, 16, body)
 
-    def weight_terms(start, count, first):
+    def weight_terms(a, start, count, first):
+        left, right = ((geps, h0), (xn0, gh0))[a]
         rows = pl.ds(start, count)
-        for a, (left, right) in enumerate(((geps, h0), (xn0, gh0))):
-            def body(i, carry):
-                cols = pl.ds(pl.multiple_of(i * 256, 256), 256)
-                term = tn(left[rows, cols], right[rows, :])
-                if first:
-                    acc[a, cols, :] = term
-                else:
-                    acc[a, cols, :] += term
-                return carry
-
-            lax.fori_loop(0, width // 256, body, None)
-
-    hidden_back(*arrived(0))
-    for step in range(1, 5):
-        gather_step(2, geps, step)
-        hidden_back(*arrived(step))
-        if step == 2:
-            weight_terms(4 * tok, 4 * tok, True)
-    weight_terms(0, 4 * tok, False)
+
+        def body(i, carry):
+            cols = pl.ds(pl.multiple_of(i * 256, 256), 256)
+            term = tn(left[rows, cols], right[rows, :])
+            if first:
+                acc[a, cols, :] = term
+            else:
+                acc[a, cols, :] += term
+            return carry
+
+        lax.fori_loop(0, width // 256, body, None)
 
     def rows_of(a, slab, j, which):
         cx, cy = (slab, j) if a == 0 else (j, slab)
@@ -428,14 +420,28 @@
 
     def core_copy(a, n):
         slab = (place[a] + (2, 1, 3, 0)[n]) % NR
-        return remote(cstg.at[a, slab], crcv.at[a, slab], c_send.at[a, n], c_recv.at[a, n], partner)
-
-    for n in range(4):
-        for a in (0, 1):
+        return remote(cstg.at[a, slab], crcv.at[a, slab], c_send, c_recv.at[a, n], partner)
+
+    def core_send(a):
+        for n in range(4):
             slab = (place[a] + (2, 1, 3, 0)[n]) % NR
             for part in (0, 1):
                 cstg[a, slab, pl.ds(80 * part, 80), :] = pair(a, slab, part, 1 - core).astype(BF16)
-            go(core_copy(a, n))
+            core_copy(a, n).start()
+
+    hidden_back(*arrived(0))
+    for step in range(1, 5):
+        gather_step(geps, step)
+        if step < 4:
+            hidden_back(*arrived(step))
+        if step == 3:
+            weight_terms(0, tok, 7 * tok, True)
+            weight_terms(1, tok, 7 * tok, True)
+    weight_terms(0, 0, tok, False)
+    core_send(0)
+    hidden_back(*arrived(4))
+    weight_terms(1, 0, tok, False)
+    core_send(1)
 
     def own_part(a, distance, part):
         slab = (place[a] + distance) % NR
@@ -446,14 +452,14 @@
         rows = pl.ds(80 * part, 80)
         return remote(
             rstg.at[a, way, step - 1, rows], rrcv.at[a, way, step - 1, rows],
-            g_send.at[at], g_recv.at[at], along[a](1 if way == 0 else -1),
+            g_send, g_recv.at[at], along[a](1 if way == 0 else -1),
         )
 
     for a in (0, 1):
         core_copy(a, 0).wait_recv()
         for way in (0, 1):
             rstg[a, way, 0, pl.ds(80 * way, 80), :] = own_part(a, 2, way).astype(BF16)
-            go(ring_copy(a, way, 1, way))
+            ring_copy(a, way, 1, way).start()
     for a in (0, 1):
         for way in (0, 1):
             core_copy(a, 1 + way).wait_recv()
@@ -463,12 +469,12 @@
                     ring_copy(a, way, 1, part).wait_recv()
                     value = value + rrcv[a, way, 0, pl.ds(80 * part, 80), :].astype(F32)
                 rstg[a, way, 1, pl.ds(80 * part, 80), :] = value.astype(BF16)
-                go(ring_copy(a, way, 2, part))
+                ring_copy(a, way, 2, part).start()
 
     def last_copy(a, k):
         target = (place[1 - a] + k) % NR
         return remote(
-            tstg.at[a, target], trcv.at[a, k - 1], t_send.at[a, k - 1], t_recv.at[a, k - 1],
+            tstg.at[a, target], trcv.at[a, k - 1], t_send, t_recv.at[a, k - 1],
             along[1 - a](k),
         )
 
@@ -486,15 +492,26 @@
                     [rows, jnp.zeros((8, hidden), F32)], axis=0
                 ).astype(BF16)
         for k in range(1, NR):
-            go(last_copy(a, k))
+            last_copy(a, k).start()
     for a, result in enumerate((gout, gin)):
         total = tsum[a, place[1 - a]]
         for k in range(1, NR):
             last_copy(a, k).wait_recv()
             total = total + trcv[a, k - 1].astype(F32)[:40]
         result[...] = total
-    for copy in pending:
-        copy.wait_send()
+    sent(lats.at[pl.ds(0, (NZ - 1) * tok)], ag_send)
+    sent(lats.at[pl.ds(0, (NZ - 1) * tok)], rs_send)
+    sent(w_in, w_send)
+    sent(idb.at[pl.ds(0, NZ - 1)], id_send)
+    sent(prcv, p_send)
+    sent(crcv, c_send)
+    sent(w_in.at[0, pl.ds(0, 960)], g_send)
+    sent(trcv, t_send)
+
+
+def hand_over(left, right, left_out, right_out):
+    left_out[...] = left[...]
+    right_out[...] = right[...]
 
 
 def on_device(latents, timesteps, prompt_ids, prompt_table, gains, w_in, w_out):
@@ -536,18 +553,18 @@
         vmem((2, NR, 40, hidden), F32),
         vmem((2, NR - 1, 48, hidden), BF16),
         dma((3,)),
-        dma((2, 8)), dma((2, 8)),
-        dma((3, 2, 8)), dma((3, 2, 8)),
-        dma((2, 2, 8)), dma((2, 2, 8)),
-        dma((7,)), dma((7,)),
-        dma((7,)), dma((7,)),
-        dma((2, 4)), dma((2, 4)),
-        dma((2, 2, 4)), dma((2, 2, 4)),
-        dma((2, 3)), dma((2, 3)),
+        dma(()), dma((2, 8)),
+        dma(()), dma((2, 4 * PARTS)),
+        dma(()), dma((2, 4 * PARTS)),
+        dma(()), dma((7,)),
+        dma(()), dma((7,)),
+        dma(()), dma((2, 4)),
+        dma(()), dma((2, 2, 4)),
+        dma(()), dma((2, 3)),
     ]
     whole, scalar, away = (pl.BlockSpec(memory_space=s) for s in (pltpu.VMEM, pltpu.SMEM, pl.ANY))
     share = jax.ShapeDtypeStruct((width // 32, hidden), F32)
-    return pl.pallas_call(
+    shares = pl.pallas_call(
         kernel,
         out_shape=(share, share),
         in_specs=[away, scalar, scalar, whole, whole, away, away],
@@ -558,6 +575,7 @@
         ),
         name="draft_step",
     )(latents, timesteps, prompt_ids, prompt_table, gains, w_in, w_out)
+    return pl.pallas_call(hand_over, out_shape=(share, share), name="hand_over")(*shares)
 
 
 def solution(mesh):

time: 147 us -> 129 us (0.88)
  Pallas kernels: 142 us -> 126 us
  local copies, waits for them, and re-layouts: 3.09 us -> 0 us
    pallas_call x1, Pallas kernels: 142 us -> 125 us  [on_device(): pl.pallas_call(kernel, out_shape=(share, share), in_specs=[away, scalar,...]
    unnamed x2 -> x0, local copies, waits for them, and re-layouts: 3.09 us -> none
    pallas_call x0 -> x1, Pallas kernels: none -> 1.63 us  [on_device(): pl.pallas_call(hand_over, out_shape=(share, share), name='hand_over')]
where the time goes in v3:
time: 129 us; the launch traced here: 127 us
  Pallas kernels  126 us (98%)
    pallas_call x1, Pallas kernels, on_device(): pl.pallas_call(kernel, out_shape=(share, share), in_specs=[away, scalar,...  125 us

profile of v3, /device:TPU:32, one launch (start us, length us, event | category | flops | bytes accessed | tf_op | source)
XLA Modules:
  0.0 126.9 jit_solution(5527624841336969633)
XLA Ops:
  0.6 124.6 %draft_step.1 = (f32[40,640]{1,0:T(8,128)}, f32[40,640]{1,0:T(8,128)}) custom-call(bf16[2,64,1280]{2,1,0:T(8,128)(2,1)} %lat.1, s32[2]{0:T(128)} %steps.1, s32[2]{0:T(128)} %ids.1, bf16[64,1280]{1,0:T(8,128)(2,1)} %table.1, f32[2,1280]{1,0:T(2,128)} %gains.1, bf16[1,1280,640]{2,1,0:T(8,128)(2,1)} %win.1, bf16[1,1280,640]{2,1,0:T(8,128)(2,1)} %wout.1), custom_call_target="tpu_custom_call" | custom-call | tf_op jit(solution)/shard_map/draft_step/pallas_call | solution.py:567
  125.2 1.6 %hand_over.1 = (f32[40,640]{1,0:T(8,128)}, f32[40,640]{1,0:T(8,128)}) custom-call(f32[40,640]{1,0:T(8,128)} %get-tuple-element.4.left, f32[40,640]{1,0:T(8,128)} %get-tuple-element.5.right), custom_call_target="tpu_custom_call" | custom-call | tf_op jit(solution)/shard_map/hand_over/pallas_call | solution.py:578

commit v4 on v3

--- a/solution.py
+++ b/solution.py
@@ -36,8 +36,8 @@
 def kernel(
     lat, steps, ids, table, gains, win, wout, gin, gout,
     w_in, w_out, lats, xn0, h0, sl0, imgs, xn1, sl1, gh1, geps, gh0, hp, pf, pf2, stg1, rcv1, stg2,
-    rcv2, idb, hm, pm, pmsg, prcv, acc, cstg, crcv, rstg, rrcv, tstg, tsum, trcv,
-    local_sem, w_send, w_recv, ag_send, ag_recv, rs_send, rs_recv, id_send, id_recv, p_send, p_recv,
+    rcv2, idb, hm, pm, pmsg, prcv, pmsg2, prcv2, acc, turned, cstg, crcv, rstg, rrcv, tstg, tsum, trcv,
+    local_sem, w_send, w_recv, ag_send, ag_recv, rs_send, rs_recv, id_send, id_recv, p_send, p_recv, p2_send, p2_recv,
     c_send, c_recv, g_send, g_recv, t_send, t_recv,
 ):
     tok, width = lat.shape[1], lat.shape[2]
@@ -89,10 +89,8 @@
     def far(part, way):
         return part // (PARTS // 2) == way
 
-    def parts_of(farthest):
-        if farthest:
-            return [(p + way * (PARTS // 2), way) for p in range(PARTS // 2) for way in (0, 1)]
-        return [(part, way) for part in range(PARTS) for way in (0, 1)]
+    far_parts = [(p + way * (PARTS // 2), way) for p in range(PARTS // 2) for way in (0, 1)]
+    near_parts = [(p + (1 - way) * (PARTS // 2), way) for p in range(PARTS // 2) for way in (0, 1)]
 
     def gather_copy(buf, way, step, part):
         if way == 0:
@@ -106,15 +104,34 @@
             ag_send, ag_recv.at[at], device,
         )
 
-    def gather_begin(buf, part):
-        for way in (0, 1):
+    def gather_begin(buf, parts):
+        for part, way in parts:
             gather_copy(buf, way, 1, part).start()
 
-    def gather_step(buf, step):
-        for part, way in parts_of(step == NZ // 2):
+    def gather_parts(buf, step, parts):
+        for part, way in parts:
             gather_copy(buf, way, step, part).wait_recv()
             if step + 1 < NZ // 2 or (step + 1 == NZ // 2 and far(part, way)):
                 gather_copy(buf, way, step + 1, part).start()
+
+    def gather_step(buf, step):
+        gather_parts(buf, step, far_parts)
+        if step < NZ // 2:
+            gather_parts(buf, step, near_parts)
+
+    def gather_with(buf, work, middle=None):
+        work(*arrived(0))
+        gather_step(buf, 1)
+        for step in (1, 2, 3):
+            start, count = arrived(step)
+            work(start, tok)
+            if step < 3:
+                gather_parts(buf, step + 1, far_parts)
+            work(start + tok, tok)
+            if step == 2 and middle is not None:
+                middle()
+            if step < 3:
+                gather_parts(buf, step + 1, near_parts)
 
     def arrived(step):
         if step == 0:
@@ -132,10 +149,7 @@
         )
 
     def scatter_step(stg, rcv, step):
-        rows = parts_of(step == 1)
-        if step == 2:
-            rows.sort(key=lambda row: far(*row))
-        for part, way in rows:
+        for part, way in (near_parts if step > 1 else []) + far_parts:
             at = pl.ds(part * size, size)
             base = part * size + (way * tok if step > 1 else 0)
             value = pf[pl.ds(base, size), :]
@@ -154,41 +168,42 @@
 
     quarter = (x + 2 * ylo) % NR
 
-    def piece(offset, which):
+    def piece(offset, which, h):
         rows = (quarter + offset) % NR * (width // NR) + which * (width // NR // 2)
-        return pl.ds(pl.multiple_of(rows, 32), width // NR // 2)
+        return pl.ds(pl.multiple_of(rows + h * (width // NR // 4), 16), width // NR // 4)
 
     held = (w_in, w_out)
     given = (win, wout)
     beside = {"dp": x * 4 + (1 - ylo) * 2 + core}
 
-    def weight_copy(a, kind):
+    def weight_copy(a, kind, h):
         if kind == 0:
-            rows = piece(2, core)
+            rows = piece(2, core, h)
             src, dst, device = given[a].at[0, rows], held[a].at[sec, rows], across
         else:
-            rows = piece((0, 0, 0, 0, 0, 3, 1, 2)[kind], core)
+            rows = piece((0, 0, 0, 0, 0, 3, 1, 2)[kind], core, h)
             src = dst = held[a].at[other, rows]
             device = (at_x(1), at_x(-1), beside, partner)[min(kind, 4) - 1]
-        return remote(src, dst, w_send, w_recv.at[a, kind], device)
-
-    def weight_landed(a, kind):
-        ref = held[a].at[other, piece((0, 3, 1, 2)[kind % 4], core if kind < 4 else 1 - core)]
-        remote(ref, ref, w_send, w_recv.at[a, kind], partner).wait_recv()
-
-    def weights_first(a):
-        weight_landed(a, 0)
+        return remote(src, dst, w_send, w_recv.at[a, kind, h], device)
+
+    def weight_landed(a, kind, h):
+        ref = held[a].at[other, piece((0, 3, 1, 2)[kind % 4], core if kind < 4 else 1 - core, h)]
+        remote(ref, ref, w_send, w_recv.at[a, kind, h], partner).wait_recv()
+
+    def weights_first(a, h):
+        weight_landed(a, 0, h)
         for kind in (1, 2, 3, 4):
-            weight_copy(a, kind).start()
-
-    def weights_second(a):
+            weight_copy(a, kind, h).start()
+
+    def weights_second(a, h):
         for kind in (1, 2, 3):
-            weight_landed(a, kind)
-            weight_copy(a, kind + 4).start()
+            weight_landed(a, kind, h)
+            weight_copy(a, kind + 4, h).start()
 
     def weights_last(a):
-        for kind in (4, 5, 6, 7):
-            weight_landed(a, kind)
+        for h in (0, 1):
+            for kind in (4, 5, 6, 7):
+                weight_landed(a, kind, h)
 
     def each(count, rows, body, init=None):
         return lax.fori_loop(0, count // rows, lambda i, c: body(pl.multiple_of(i * rows, rows), c), init)
@@ -215,25 +230,30 @@
         math.pi / 2.0 / (STEPS + 1.0)
     )
     alpha, sigma = jnp.cos(theta)[:, :1], jnp.sin(theta)[:, :1]
-    weight_copy(0, 0).start()
-    weight_copy(1, 0).start()
+    for a in (0, 1):
+        for h in (0, 1):
+            weight_copy(a, 0, h).start()
     here[0].wait()
-    for part in range(PARTS):
-        gather_begin(lats, part)
+    gather_begin(lats, far_parts + near_parts)
     for k in range(1, NZ):
         remote(idb.at[0], idb.at[k], id_send, id_recv.at[k - 1], at_z(k)).start()
     gain0, gain1 = gains[0:1, :], gains[1:2, :]
     norm(lats, xn0, *arrived(0), gain0)
     gather_step(lats, 1)
-    weights_first(0)
+    weights_first(0, 0)
     norm(lats, xn0, *arrived(1), gain0)
+    weights_first(0, 1)
     gather_step(lats, 2)
+    weights_first(1, 0)
+    weights_second(0, 0)
     norm(lats, xn0, *arrived(2), gain0)
-    weights_first(1)
+    weights_first(1, 1)
+    weights_second(0, 1)
     gather_step(lats, 3)
-    weights_second(0)
+    weights_second(1, 0)
     norm(lats, xn0, *arrived(3), gain0)
     gather_step(lats, 4)
+    weights_second(1, 1)
     norm(lats, xn0, *arrived(4), gain0)
     here[1].wait()
     weights_last(0)
@@ -252,14 +272,12 @@
         each(count, 16, body)
 
     hidden0(*chunk(1))
-    weights_second(1)
-    hidden0(*chunk(2))
     here[2].wait()
     weights_last(1)
 
     for step in range(1, 6):
         start, count = chunk(step)
-        if step > 2:
+        if step > 1:
             hidden0(start, count)
         out = nt(h0[pl.ds(start, count), :], w_out[0])
         if step < 5:
@@ -270,7 +288,7 @@
 
     own = POS[0] * tok
     sent(lats.at[pl.ds(0, (NZ - 1) * tok)], ag_send)
-    for part in range(PARTS):
+    for part, way in far_parts:
         scatter_end(stg1, rcv1, part)
 
         def images(at, carry):
@@ -283,7 +301,9 @@
             return carry
 
         each(size, 16, images)
-        gather_begin(imgs, part)
+        gather_begin(imgs, [(part, way)])
+
+    gather_begin(imgs, near_parts)
 
     def hidden1(start, count):
         slots = slots_of(start, count)
@@ -301,7 +321,6 @@
             total = each(tok, 16, body, jnp.zeros((8, hidden), F32))
             hm[pl.ds(slot, 1), :] = jnp.sum(total, axis=0, keepdims=True) * (1.0 / tok)
 
-    hidden1(*arrived(0))
     for k in range(1, NZ):
         remote(idb.at[k], idb.at[k], id_send, id_recv.at[k - 1], at_z(k)).wait_recv()
     id_rows = jnp.concatenate([idb[k, 0:1, :] for k in range(NZ)], axis=0)
@@ -311,25 +330,46 @@
     ).astype(F32).astype(BF16)
     text = jnp.dot(onehot, table[...], preferred_element_type=F32)
     text = text * lax.rsqrt(jnp.mean(text * text, axis=-1, keepdims=True) + EPS)
-    for step in range(1, 5):
-        gather_step(imgs, step)
-        hidden1(*arrived(step))
-
-    mean1 = hm[...]
-    high = mean1.astype(BF16).astype(F32)
-    both = jnp.concatenate([high, mean1 - high], axis=0).astype(BF16)
-    mixed = nt(both, w_out[1])
-    mixed = mixed[:NZ] + mixed[NZ:]
+    def mixed_rows(rows):
+        high = rows.astype(BF16).astype(F32)
+        both = jnp.concatenate([high, rows - high], axis=0).astype(BF16)
+        out = nt(both, w_out[1])
+        return out[:NZ] + out[NZ:]
+
+    def exchange(message, arrivals, send_sem, recv_sem, k):
+        return remote(message, arrivals.at[k - 1], send_sem, recv_sem.at[k - 1], at_z(k))
+
     mid = width // 2
+    opposite = NZ // 2
+    hm[pl.ds(opposite, 1), :] = jnp.zeros((1, hidden), F32)
+    gather_with(imgs, hidden1)
+    mixed = mixed_rows(hm[...])
     pmsg[...] = jnp.concatenate([mixed[:, :mid], mixed[:, mid:]], axis=0).astype(BF16)
     for k in range(1, NZ):
-        remote(pmsg, prcv.at[k - 1], p_send, p_recv.at[k - 1], at_z(k)).start()
+        exchange(pmsg, prcv, p_send, p_recv, k).start()
+    gather_parts(imgs, 4, far_parts)
+    hidden1(*arrived(4))
+
+    lanes = width // 128
+    last = mixed_rows(jnp.broadcast_to(hm[pl.ds(opposite, 1), :], (NZ, hidden)))[0:1]
+    pmsg2[...] = jnp.concatenate(
+        [last[:, 128 * i:128 * i + 128] for i in range(lanes)] + [jnp.zeros((16 - lanes, 128), F32)],
+        axis=0,
+    ).astype(BF16)
+    for k in range(1, NZ):
+        exchange(pmsg2, prcv2, p2_send, p2_recv, k).start()
     pooled = pm[...] + mixed
     for k in range(1, NZ):
-        remote(pmsg, prcv.at[k - 1], p_send, p_recv.at[k - 1], at_z(k)).wait_recv()
+        exchange(pmsg, prcv, p_send, p_recv, k).wait_recv()
         got = prcv[k - 1].astype(F32)
         got = jnp.concatenate([got[:NZ], got[NZ:]], axis=1)
         pooled = pooled + jnp.concatenate([got[NZ - k:], got[:NZ - k]], axis=0)
+    rows = {opposite: last}
+    for k in range(1, NZ):
+        exchange(pmsg2, prcv2, p2_send, p2_recv, k).wait_recv()
+        got = prcv2[k - 1].astype(F32)
+        rows[(opposite + k) % NZ] = jnp.concatenate([got[i:i + 1] for i in range(lanes)], axis=1)
+    pooled = pooled + jnp.concatenate([rows[k] for k in range(NZ)], axis=0)
     unit = lax.rsqrt(jnp.mean(pooled * pooled, axis=-1, keepdims=True) + EPS)
     g_mean = (unit * text - pooled * (unit * unit * unit) * jnp.mean(
         pooled * text, axis=-1, keepdims=True
@@ -358,7 +398,7 @@
 
     ratio = -(sigma / alpha)
     sent(lats.at[pl.ds(0, (NZ - 1) * tok)], ag_send)
-    for part in range(PARTS):
+    for part, way in far_parts:
         scatter_end(stg2, rcv2, part)
 
         def back(at, carry):
@@ -377,7 +417,9 @@
             return carry
 
         each(size, 16, back)
-        gather_begin(geps, part)
+        gather_begin(geps, [(part, way)])
+
+    gather_begin(geps, near_parts)
 
     def hidden_back(start, count):
         hp[pl.ds(0, count), :] = jnp.dot(
@@ -422,26 +464,32 @@
         slab = (place[a] + (2, 1, 3, 0)[n]) % NR
         return remote(cstg.at[a, slab], crcv.at[a, slab], c_send, c_recv.at[a, n], partner)
 
-    def core_send(a):
-        for n in range(4):
-            slab = (place[a] + (2, 1, 3, 0)[n]) % NR
-            for part in (0, 1):
-                cstg[a, slab, pl.ds(80 * part, 80), :] = pair(a, slab, part, 1 - core).astype(BF16)
-            core_copy(a, n).start()
-
-    hidden_back(*arrived(0))
-    for step in range(1, 5):
-        gather_step(geps, step)
-        if step < 4:
-            hidden_back(*arrived(step))
-        if step == 3:
-            weight_terms(0, tok, 7 * tok, True)
-            weight_terms(1, tok, 7 * tok, True)
-    weight_terms(0, 0, tok, False)
-    core_send(0)
+    def early_terms():
+        weight_terms(0, 4 * tok, 4 * tok, True)
+        weight_terms(1, 4 * tok, 4 * tok, True)
+
+    def slab_terms(a, n):
+        slab = (place[a] + (2, 1, 3, 0)[n]) % NR
+        if a == 0:
+            blocks = [(s * 640 + slab * 160, 160) for s in (0, 1)]
+        else:
+            blocks = [((slab // 2) * 640 + cx * 160 + (slab % 2) * 80, 80) for cx in range(NR)]
+        right = (h0, gh0)[a][pl.ds(0, 4 * tok), :]
+        for start, count in blocks:
+            rows = pl.ds(pl.multiple_of(start, 16), count)
+            acc[a, rows, :] += jnp.dot(turned[a, rows, :], right, preferred_element_type=F32)
+        for part in (0, 1):
+            cstg[a, slab, pl.ds(80 * part, 80), :] = pair(a, slab, part, 1 - core).astype(BF16)
+        core_copy(a, n).start()
+
+    turned[1] = xn0[pl.ds(0, 4 * tok), :].T
+    gather_with(geps, hidden_back, early_terms)
+    gather_parts(geps, 4, far_parts)
+    turned[0] = geps[pl.ds(0, 4 * tok), :].T
+    slab_terms(0, 0)
     hidden_back(*arrived(4))
-    weight_terms(1, 0, tok, False)
-    core_send(1)
+    for a, n in ((1, 0), (0, 1), (1, 1), (0, 2), (1, 2)):
+        slab_terms(a, n)
 
     def own_part(a, distance, part):
         slab = (place[a] + distance) % NR
@@ -455,21 +503,28 @@
             g_send, g_recv.at[at], along[a](1 if way == 0 else -1),
         )
 
+    def ring_send(a, way, step, part):
+        distance = 2 if step == 1 else (1 if way == 0 else 3)
+        value = own_part(a, distance, part)
+        if step == 2 and part == way:
+            ring_copy(a, way, 1, part).wait_recv()
+            value = value + rrcv[a, way, 0, pl.ds(80 * part, 80), :].astype(F32)
+        rstg[a, way, step - 1, pl.ds(80 * part, 80), :] = value.astype(BF16)
+        ring_copy(a, way, step, part).start()
+
     for a in (0, 1):
         core_copy(a, 0).wait_recv()
         for way in (0, 1):
-            rstg[a, way, 0, pl.ds(80 * way, 80), :] = own_part(a, 2, way).astype(BF16)
-            ring_copy(a, way, 1, way).start()
+            ring_send(a, way, 1, way)
+    for way in (0, 1):
+        for a in (0, 1):
+            core_copy(a, 1 + way).wait_recv()
+            ring_send(a, way, 2, 1 - way)
+    for a in (0, 1):
+        slab_terms(a, 3)
     for a in (0, 1):
         for way in (0, 1):
-            core_copy(a, 1 + way).wait_recv()
-            for part in (1 - way, way):
-                value = own_part(a, 1 if way == 0 else 3, part)
-                if part == way:
-                    ring_copy(a, way, 1, part).wait_recv()
-                    value = value + rrcv[a, way, 0, pl.ds(80 * part, 80), :].astype(F32)
-                rstg[a, way, 1, pl.ds(80 * part, 80), :] = value.astype(BF16)
-                ring_copy(a, way, 2, part).start()
+            ring_send(a, way, 2, way)
 
     def last_copy(a, k):
         target = (place[1 - a] + k) % NR
@@ -504,6 +559,7 @@
     sent(w_in, w_send)
     sent(idb.at[pl.ds(0, NZ - 1)], id_send)
     sent(prcv, p_send)
+    sent(prcv2, p2_send)
     sent(crcv, c_send)
     sent(w_in.at[0, pl.ds(0, 960)], g_send)
     sent(trcv, t_send)
@@ -544,7 +600,10 @@
         vmem((NZ, width), F32),
         vmem((2 * NZ, width // 2), BF16),
         vmem((NZ - 1, 2 * NZ, width // 2), BF16),
+        vmem((16, 128), BF16),
+        vmem((NZ - 1, 16, 128), BF16),
         vmem((2, width, hidden), F32),
+        vmem((2, width, rows // 2), BF16),
         vmem((2, NR, 160, hidden), BF16),
         vmem((2, NR, 160, hidden), BF16),
         vmem((2, 2, 2, 160, hidden), BF16),
@@ -553,9 +612,10 @@
         vmem((2, NR, 40, hidden), F32),
         vmem((2, NR - 1, 48, hidden), BF16),
         dma((3,)),
-        dma(()), dma((2, 8)),
+        dma(()), dma((2, 8, 2)),
         dma(()), dma((2, 4 * PARTS)),
         dma(()), dma((2, 4 * PARTS)),
+        dma(()), dma((7,)),
         dma(()), dma((7,)),
         dma(()), dma((7,)),
         dma(()), dma((2, 4)),

time: 129 us -> 121 us (0.938); the launches traced: 127 us -> 120 us
  Pallas kernels: 126 us -> 120 us
    pallas_call x1, Pallas kernels: 125 us -> 118 us  [on_device(): pl.pallas_call(kernel, out_shape=(share, share), in_specs=[away, scalar,...]
where the time goes in v4:
time: 121 us; the launch traced here: 120 us
  Pallas kernels  120 us (99%)
    pallas_call x1, Pallas kernels, on_device(): pl.pallas_call(kernel, out_shape=(share, share), in_specs=[away, scalar,...  118 us

profile of v4, /device:TPU:32, one launch (start us, length us, event | category | flops | bytes accessed | tf_op | source)
XLA Modules:
  0.0 120.3 jit_solution(1746816141969856685)
XLA Ops:
  0.6 118.0 %draft_step.1 = (f32[40,640]{1,0:T(8,128)}, f32[40,640]{1,0:T(8,128)}) custom-call(bf16[2,64,1280]{2,1,0:T(8,128)(2,1)} %lat.1, s32[2]{0:T(128)} %steps.1, s32[2]{0:T(128)} %ids.1, bf16[64,1280]{1,0:T(8,128)(2,1)} %table.1, f32[2,1280]{1,0:T(2,128)} %gains.1, bf16[1,1280,640]{2,1,0:T(8,128)(2,1)} %win.1, bf16[1,1280,640]{2,1,0:T(8,128)(2,1)} %wout.1), custom_call_target="tpu_custom_call" | custom-call | tf_op jit(solution)/shard_map/draft_step/pallas_call | solution.py:627
  118.6 1.6 %hand_over.1 = (f32[40,640]{1,0:T(8,128)}, f32[40,640]{1,0:T(8,128)}) custom-call(f32[40,640]{1,0:T(8,128)} %get-tuple-element.4.left, f32[40,640]{1,0:T(8,128)} %get-tuple-element.5.right), custom_call_target="tpu_custom_call" | custom-call | tf_op jit(solution)/shard_map/hand_over/pallas_call | solution.py:638

commit v5 on v4

--- a/solution.py
+++ b/solution.py
@@ -16,6 +16,7 @@
 ORDER = (4, 5, 3, 6, 2, 7, 1, 0)
 POS = {slot: pos for pos, slot in enumerate(ORDER)}
 NZ, NR = 8, 4
+FAR_FIRST = (4, 3, 5, 2, 6, 1, 7)
 PARTS = 4
 
 
@@ -79,8 +80,7 @@
         copy.start()
     idb[0] = jnp.full((8, 128), ids[sec], jnp.int32)
 
-    peers = [at_z(k) for k in range(1, NZ)] + [partner]
-    peers += [at_x(k) for k in range(1, NR)] + [at_y(k) for k in range(1, NR)]
+    peers = [at(k) for at in (at_z, at_x, at_y) for k in (1, -1)] + [partner]
     barrier = pltpu.get_barrier_semaphore()
     for peer in peers:
         pl.semaphore_signal(barrier, inc=1, device_id=peer, device_id_type=MESH)
@@ -235,8 +235,6 @@
             weight_copy(a, 0, h).start()
     here[0].wait()
     gather_begin(lats, far_parts + near_parts)
-    for k in range(1, NZ):
-        remote(idb.at[0], idb.at[k], id_send, id_recv.at[k - 1], at_z(k)).start()
     gain0, gain1 = gains[0:1, :], gains[1:2, :]
     norm(lats, xn0, *arrived(0), gain0)
     gather_step(lats, 1)
@@ -254,6 +252,8 @@
     norm(lats, xn0, *arrived(3), gain0)
     gather_step(lats, 4)
     weights_second(1, 1)
+    for k in range(1, NZ):
+        remote(idb.at[0], idb.at[k], id_send, id_recv.at[k - 1], at_z(k)).start()
     norm(lats, xn0, *arrived(4), gain0)
     here[1].wait()
     weights_last(0)
@@ -345,7 +345,7 @@
     gather_with(imgs, hidden1)
     mixed = mixed_rows(hm[...])
     pmsg[...] = jnp.concatenate([mixed[:, :mid], mixed[:, mid:]], axis=0).astype(BF16)
-    for k in range(1, NZ):
+    for k in FAR_FIRST:
         exchange(pmsg, prcv, p_send, p_recv, k).start()
     gather_parts(imgs, 4, far_parts)
     hidden1(*arrived(4))
@@ -356,7 +356,7 @@
         [last[:, 128 * i:128 * i + 128] for i in range(lanes)] + [jnp.zeros((16 - lanes, 128), F32)],
         axis=0,
     ).astype(BF16)
-    for k in range(1, NZ):
+    for k in FAR_FIRST:
         exchange(pmsg2, prcv2, p2_send, p2_recv, k).start()
     pooled = pm[...] + mixed
     for k in range(1, NZ):
@@ -546,7 +546,7 @@
                 tstg[a, 2 * part + j] = jnp.concatenate(
                     [rows, jnp.zeros((8, hidden), F32)], axis=0
                 ).astype(BF16)
-        for k in range(1, NR):
+        for k in (2, 1, 3):
             last_copy(a, k).start()
     for a, result in enumerate((gout, gin)):
         total = tsum[a, place[1 - a]]

time: 121 us -> 120 us (level)
  Pallas kernels: 120 us -> 118 us
    pallas_call x1, Pallas kernels: 118 us -> 117 us  [on_device(): pl.pallas_call(kernel, out_shape=(share, share), in_specs=[away, scalar,...]
where the time goes in v5:
time: 120 us; the launch traced here: 119 us
  Pallas kernels  118 us (98%)
    pallas_call x1, Pallas kernels, on_device(): pl.pallas_call(kernel, out_shape=(share, share), in_specs=[away, scalar,...  117 us

profile of v5, /device:TPU:32, one launch (start us, length us, event | category | flops | bytes accessed | tf_op | source)
XLA Modules:
  0.0 119.0 jit_solution(2146170868030066281)
XLA Ops:
  0.6 116.7 %draft_step.1 = (f32[40,640]{1,0:T(8,128)}, f32[40,640]{1,0:T(8,128)}) custom-call(bf16[2,64,1280]{2,1,0:T(8,128)(2,1)} %lat.1, s32[2]{0:T(128)} %steps.1, s32[2]{0:T(128)} %ids.1, bf16[64,1280]{1,0:T(8,128)(2,1)} %table.1, f32[2,1280]{1,0:T(2,128)} %gains.1, bf16[1,1280,640]{2,1,0:T(8,128)(2,1)} %win.1, bf16[1,1280,640]{2,1,0:T(8,128)(2,1)} %wout.1), custom_call_target="tpu_custom_call" | custom-call | tf_op jit(solution)/shard_map/draft_step/pallas_call | solution.py:627
  117.3 1.6 %hand_over.1 = (f32[40,640]{1,0:T(8,128)}, f32[40,640]{1,0:T(8,128)}) custom-call(f32[40,640]{1,0:T(8,128)} %get-tuple-element.4.left, f32[40,640]{1,0:T(8,128)} %get-tuple-element.5.right), custom_call_target="tpu_custom_call" | custom-call | tf_op jit(solution)/shard_map/hand_over/pallas_call | solution.py:638

commit v6 on v5

--- a/solution.py
+++ b/solution.py
@@ -206,7 +206,14 @@
                 weight_landed(a, kind, h)
 
     def each(count, rows, body, init=None):
-        return lax.fori_loop(0, count // rows, lambda i, c: body(pl.multiple_of(i * rows, rows), c), init)
+        several = min(4, count // rows)
+
+        def group(i, carry):
+            for j in range(several):
+                carry = body(pl.multiple_of((i * several + j) * rows, rows), carry)
+            return carry
+
+        return lax.fori_loop(0, count // rows // several, group, init)
 
     def norm(buf, dst, start, count, gain, slots=None):
         def body(at, total):
@@ -433,20 +440,13 @@
 
         each(count, 16, body)
 
-    def weight_terms(a, start, count, first):
+    def weight_terms(a, start, count):
         left, right = ((geps, h0), (xn0, gh0))[a]
         rows = pl.ds(start, count)
 
-        def body(i, carry):
-            cols = pl.ds(pl.multiple_of(i * 256, 256), 256)
-            term = tn(left[rows, cols], right[rows, :])
-            if first:
-                acc[a, cols, :] = term
-            else:
-                acc[a, cols, :] += term
-            return carry
-
-        lax.fori_loop(0, width // 256, body, None)
+        for i in range(width // 256):
+            cols = pl.ds(i * 256, 256)
+            acc[a, cols, :] = tn(left[rows, cols], right[rows, :])
 
     def rows_of(a, slab, j, which):
         cx, cy = (slab, j) if a == 0 else (j, slab)
@@ -465,8 +465,8 @@
         return remote(cstg.at[a, slab], crcv.at[a, slab], c_send, c_recv.at[a, n], partner)
 
     def early_terms():
-        weight_terms(0, 4 * tok, 4 * tok, True)
-        weight_terms(1, 4 * tok, 4 * tok, True)
+        weight_terms(0, 4 * tok, 4 * tok)
+        weight_terms(1, 4 * tok, 4 * tok)
 
     def slab_terms(a, n):
         slab = (place[a] + (2, 1, 3, 0)[n]) % NR

time: 120 us -> 118 us (0.983)
  Pallas kernels: 118 us -> 116 us
    pallas_call x1, Pallas kernels: 117 us -> 114 us  [on_device(): pl.pallas_call(kernel, out_shape=(share, share), in_specs=[away, scalar,...]
where the time goes in v6:
time: 118 us; the launch traced here: 116 us
  Pallas kernels  116 us (98%)
    pallas_call x1, Pallas kernels, on_device(): pl.pallas_call(kernel, out_shape=(share, share), in_specs=[away, scalar,...  114 us

profile of v6, /device:TPU:32, one launch (start us, length us, event | category | flops | bytes accessed | tf_op | source)
XLA Modules:
  0.0 116.4 jit_solution(15155415523095796865)
XLA Ops:
  0.6 114.1 %draft_step.1 = (f32[40,640]{1,0:T(8,128)}, f32[40,640]{1,0:T(8,128)}) custom-call(bf16[2,64,1280]{2,1,0:T(8,128)(2,1)} %lat.1, s32[2]{0:T(128)} %steps.1, s32[2]{0:T(128)} %ids.1, bf16[64,1280]{1,0:T(8,128)(2,1)} %table.1, f32[2,1280]{1,0:T(2,128)} %gains.1, bf16[1,1280,640]{2,1,0:T(8,128)(2,1)} %win.1, bf16[1,1280,640]{2,1,0:T(8,128)(2,1)} %wout.1), custom_call_target="tpu_custom_call" | custom-call | tf_op jit(solution)/shard_map/draft_step/pallas_call | solution.py:627
  114.8 1.6 %hand_over.1 = (f32[40,640]{1,0:T(8,128)}, f32[40,640]{1,0:T(8,128)}) custom-call(f32[40,640]{1,0:T(8,128)} %get-tuple-element.4.left, f32[40,640]{1,0:T(8,128)} %get-tuple-element.5.right), custom_call_target="tpu_custom_call" | custom-call | tf_op jit(solution)/shard_map/hand_over/pallas_call | solution.py:638

commit v7 on v6

--- a/solution.py
+++ b/solution.py
@@ -122,16 +122,15 @@
     def gather_with(buf, work, middle=None):
         work(*arrived(0))
         gather_step(buf, 1)
-        for step in (1, 2, 3):
+        for step in (1, 2):
             start, count = arrived(step)
             work(start, tok)
-            if step < 3:
-                gather_parts(buf, step + 1, far_parts)
+            gather_parts(buf, step + 1, far_parts)
             work(start + tok, tok)
             if step == 2 and middle is not None:
                 middle()
-            if step < 3:
-                gather_parts(buf, step + 1, near_parts)
+            gather_parts(buf, step + 1, near_parts)
+        work(*arrived(3))
 
     def arrived(step):
         if step == 0:
@@ -405,6 +404,8 @@
 
     ratio = -(sigma / alpha)
     sent(lats.at[pl.ds(0, (NZ - 1) * tok)], ag_send)
+    seen_own = imgs[pl.ds(own, tok), :].astype(F32)
+    scales = lax.rsqrt(jnp.mean(seen_own * seen_own, axis=-1, keepdims=True) + EPS)
     for part, way in far_parts:
         scatter_end(stg2, rcv2, part)
 
@@ -414,7 +415,7 @@
             g_xn = pf2[rows, :] + (
                 rcv2[0, 3, rows, :].astype(F32) + rcv2[1, 3, rows, :].astype(F32)
             )
-            scale = lax.rsqrt(jnp.mean(seen * seen, axis=-1, keepdims=True) + EPS)
+            scale = scales[part * size:part * size + size]
             weighted = gain1 * g_xn
             g_norm = scale * weighted - seen * (scale * scale * scale) * jnp.mean(
                 seen * weighted, axis=-1, keepdims=True

time: 118 us -> 117 us (level)
  no operation moved by 1% of the time
where the time goes in v7:
time: 117 us; the launch traced here: 116 us
  Pallas kernels  116 us (99%)
    pallas_call x1, Pallas kernels, on_device(): pl.pallas_call(kernel, out_shape=(share, share), in_specs=[away, scalar,...  114 us

profile of v7, /device:TPU:32, one launch (start us, length us, event | category | flops | bytes accessed | tf_op | source)
XLA Modules:
  0.0 116.4 jit_solution(15907380955609155778)
XLA Ops:
  0.6 114.2 %draft_step.1 = (f32[40,640]{1,0:T(8,128)}, f32[40,640]{1,0:T(8,128)}) custom-call(bf16[2,64,1280]{2,1,0:T(8,128)(2,1)} %lat.1, s32[2]{0:T(128)} %steps.1, s32[2]{0:T(128)} %ids.1, bf16[64,1280]{1,0:T(8,128)(2,1)} %table.1, f32[2,1280]{1,0:T(2,128)} %gains.1, bf16[1,1280,640]{2,1,0:T(8,128)(2,1)} %win.1, bf16[1,1280,640]{2,1,0:T(8,128)(2,1)} %wout.1), custom_call_target="tpu_custom_call" | custom-call | tf_op jit(solution)/shard_map/draft_step/pallas_call | solution.py:628
  114.8 1.6 %hand_over.1 = (f32[40,640]{1,0:T(8,128)}, f32[40,640]{1,0:T(8,128)}) custom-call(f32[40,640]{1,0:T(8,128)} %get-tuple-element.4.left, f32[40,640]{1,0:T(8,128)} %get-tuple-element.5.right), custom_call_target="tpu_custom_call" | custom-call | tf_op jit(solution)/shard_map/hand_over/pallas_call | solution.py:639
